TPU v7x, 512 devices: a whole 4x4x16 slice. The times are simulated.
512 devices in a mesh: gx: 16 (over y, z_lo), gy: 4 (over z_hi), gz: 8 (over x, core).
Axes of the slice: x: 4, y: 4, z: 16 (z_hi: 4, z_lo: 4; z = z_hi * 4 + z_lo), core: 2. Of those that a mesh axis runs over, the one named last changes fastest.
Arguments:
- ref_image: bfloat16 [4096, 64, 1024], P('gx', 'gy', 'gz'), may hold values from -6 to 6
- def_image: bfloat16 [4096, 64, 1024], P('gx', 'gy', 'gz'), may hold values from -6 to 6
- displacement: float32 [3, 512, 8, 128], P(None, 'gx', 'gy', 'gz'), may hold values from -3 to 3
Outputs:
- new_displacement: float32 [3, 512, 8, 128], P(None, 'gx', 'gy', 'gz')
- fine_residual: bfloat16 [4096, 64, 1024], P('gx', 'gy', 'gz')
All inputs are finite; a program needn't handle non-finite values.
Results may differ from a plain program's by a relative error of at most 0.0022.
Values may be sent and summed in bfloat16 or wider, within the bound.
No kernel may reach another device: no remote copies, remote signals or barrier semaphores. Data moves between devices by JAX's collectives and lax.ppermute only.
A program may use at most 64 MiB of HBM per device.

v0:
```python
import jax
import jax.numpy as jnp
from jax import lax
from jax.sharding import PartitionSpec as P

stiffness = 64.0


def padded_2(cells, sides, width):
    for axis, dim in sides:
        count = lax.axis_size(axis)
        ends = count - 1
        head = lax.slice_in_dim(cells, 0, width, axis=dim)
        tail = lax.slice_in_dim(cells, cells.shape[dim] - width, cells.shape[dim], axis=dim)
        cells = jnp.concatenate(
            [
                lax.ppermute(tail, axis, [(i, (i + 1) % count) for i in range(ends)]),
                cells,
                lax.ppermute(head, axis, [((i + 1) % count, i) for i in range(ends)]),
            ],
            axis=dim,
        )
    return cells


def in_order(parts, dim):
    shape = list(parts.shape[1:])
    shape[dim] *= parts.shape[0]
    return jnp.moveaxis(parts, 0, dim).reshape(shape)


def copy_for_each(shard, axis):
    copies = jnp.broadcast_to(shard, (lax.axis_size(axis), *shard.shape))
    return lax.all_to_all(copies, axis, split_axis=0, concat_axis=0, tiled=True)


def gather_directly(shard, axis, dim):
    return in_order(copy_for_each(shard, axis), dim)


def extended(shard, sides, width):
    edges = {}
    for axis, dim in sides:
        devices, length = (lax.axis_size(axis), shard.shape[dim])
        up = [(i, (i + 1) % devices) for i in range(devices - 1)]
        last = lax.slice_in_dim(shard, length - width, length, axis=dim)
        initial = lax.slice_in_dim(shard, 0, width, axis=dim)
        edges[dim] = (
            lax.ppermute(last, axis, up),
            lax.ppermute(initial, axis, [(b, a) for a, b in up]),
        )
    done = []
    for _, dim in sides:
        low, high = edges[dim]
        around = [(width, width) if d in done else (0, 0) for d in range(shard.ndim)]
        shard = jnp.concatenate([jnp.pad(low, around), shard, jnp.pad(high, around)], axis=dim)
        done.append(dim)
    return shard


def bin_level(image, summer):
    sizex, sizey, sizez = image.shape
    along_z = jnp.dot(
        image.reshape(sizex * sizey, sizez), summer, preferred_element_type=jnp.float32
    )
    return along_z.reshape(sizex // 8, 8, sizey // 8, 8, sizez // 8).sum((1, 3)) / 32.0


def central(padded):
    slope_x = (padded[2:, 1:-1, 1:-1] - padded[:-2, 1:-1, 1:-1]) / 2.0
    slope_y = (padded[1:-1, 2:, 1:-1] - padded[1:-1, :-2, 1:-1]) / 2.0
    slope_z = (padded[1:-1, 1:-1, 2:] - padded[1:-1, 1:-1, :-2]) / 2.0
    return (slope_x, slope_y, slope_z)


def line_matrix(count):
    return jnp.eye(count, dtype=jnp.float32) * (1.0 + 2.0 * stiffness) - stiffness * (
        jnp.eye(count, k=1, dtype=jnp.float32) + jnp.eye(count, k=-1, dtype=jnp.float32)
    )


def prolong_table(fine_count, coarse_count):
    index = jnp.arange(fine_count)
    center = index // 8 + 1
    offset = ((index % 8).astype(jnp.float32) + 0.5) / 8.0 - 0.5
    column = jnp.arange(coarse_count + 2)[None, :]
    weight = jnp.where(column == center[:, None], 1.0 - jnp.abs(offset)[:, None], 0.0)
    weight = weight + jnp.where(
        (offset[:, None] >= 0.0) & (column == center[:, None] + 1), offset[:, None], 0.0
    )
    weight = weight + jnp.where(
        (offset[:, None] < 0.0) & (column == center[:, None] - 1), -offset[:, None], 0.0
    )
    return weight


def line_solve(factor, rhs):
    items, lines, rest = rhs.shape
    flat = jnp.moveaxis(rhs, 1, 0).reshape(lines, items * rest)
    solved = jax.scipy.linalg.cho_solve((factor, True), flat)
    return jnp.moveaxis(solved.reshape(lines, items, rest), 0, 1)


def on_device(ref_image, def_image, displacement):
    sizex, sizey, sizez = ref_image.shape
    cells_x, cells_y, cells_z = (sizex // 8, sizey // 8, sizez // 8)
    summer = (jnp.arange(sizez)[:, None] // 8 == jnp.arange(cells_z)[None, :]).astype(jnp.bfloat16)
    coarse_ref = bin_level(ref_image, summer)
    coarse_def = bin_level(def_image, summer)
    ref_padded = padded_2(coarse_ref, (("gx", 0), ("gy", 1), ("gz", 2)), 1)
    slopes = central(ref_padded)
    mismatch = (
        coarse_def
        - coarse_ref
        - (slopes[0] * displacement[0] + slopes[1] * displacement[1] + slopes[2] * displacement[2])
    )
    rhs = jnp.stack([slope * mismatch for slope in slopes]).reshape(3, cells_x, cells_y * cells_z)
    lines = cells_x * lax.axis_size("gx")
    factor = jnp.linalg.cholesky(line_matrix(lines))
    whole = gather_directly(rhs, "gx", 1)
    solved = line_solve(factor, whole)
    step = lax.dynamic_slice_in_dim(solved, lax.axis_index("gx") * cells_x, cells_x, 1)
    new_displacement = displacement + step.reshape(3, cells_x, cells_y, cells_z)
    padded = padded_2(new_displacement, (("gx", 1), ("gy", 2), ("gz", 3)), 1)
    table_x = prolong_table(sizex, cells_x)
    table_y = prolong_table(sizey, cells_y)
    table_z = prolong_table(sizez, cells_z)
    field = jnp.einsum("ia,nabc->nibc", table_x, padded, precision=lax.Precision.HIGHEST)
    field = jnp.einsum("jb,nibc->nijc", table_y, field, precision=lax.Precision.HIGHEST)
    field = jnp.einsum("nijc,kc->nijk", field, table_z, precision=lax.Precision.HIGHEST)
    fine_padded = extended(ref_image, (("gx", 0), ("gy", 1), ("gz", 2)), 1)
    grads = central(fine_padded.astype(jnp.float32))
    total = def_image.astype(jnp.float32) - ref_image.astype(jnp.float32)
    total = total - grads[0] * field[0] - grads[1] * field[1] - grads[2] * field[2]
    return (new_displacement, total.astype(jnp.bfloat16))


def solution(mesh):
    return jax.shard_map(
        on_device,
        mesh=mesh,
        in_specs=(P("gx", "gy", "gz"), P("gx", "gy", "gz"), P(None, "gx", "gy", "gz")),
        out_specs=(P(None, "gx", "gy", "gz"), P("gx", "gy", "gz")),
        check_vma=False,
    )
```

profile of v0, /device:TPU:18, one launch (start us, length us, event | category | flops | bytes accessed | tf_op | source)
XLA Modules:
  0.0 301.5 jit_solution(12949534668097423135)
XLA Ops:
  0.6 1.5 copy.116
  2.8 3.8 %collective-permute-start.8 = (bf16[1,16,128]{2,0,1:T(2,128)(2,1)}, bf16[1,16,128]{2,0,1:T(2,128)(2,1)}, u32[]{:S(2)}, u32[]{:S(2)}) collective-permute-start(bf16[1,16,128]{2,0,1:T(2,128)(2,1)} %get-tuple-element.34), channel_id=1, source_target_pairs={{0,32},{32,64},{64,96},{96,128},{128,160},{160,192},{192,224},{224... | collective-permute-start | bytes 12296 | tf_op jit(solution)/shard_map/ppermute | solution.py:49
  7.2 1.7 convolution_bitcast_fusion.1
  9.9 4.7 %collective-permute-start = (f32[1,2,16]{0,2,1:T(8,128)S(1)}, f32[1,2,16]{0,2,1:T(8,128)S(1)}, u32[]{:S(2)}, u32[]{:S(2)}) collective-permute-start(f32[1,2,16]{0,2,1:T(8,128)S(1)} %get-tuple-element.64), channel_id=1, source_target_pairs={{32,0},{64,32},{96,64},{128,96},{160,128},{192,160},{224,192},{256... | collective-permute-start | bytes 392 | tf_op jit(solution)/shard_map/ppermute | solution.py:19
  14.6 1.9 collective-permute-start.1
  17.1 1.5 copy.133
  18.5 1.9 collective-permute-start.11
  20.5 1.5 copy.132
  22.0 2.7 collective-permute-start.6
  29.8 11.7 %cholesky.103 = f32[128,128]{1,0:T(8,128)S(1)} custom-call(f32[128,128]{1,0:T(8,128)S(1)} %cholesky.263), custom_call_target="Cholesky" | custom-call | tf_op jit(solution)/shard_map/jit(cholesky)/cholesky | solution.py:119
  44.6 9.8 %custom-call.34 = f32[1,128,128]{1,2,0:T(8,128)S(1)} custom-call(f32[1,128,128]{2,1,0:T(8,128)S(1)} %get-tuple-element.55), custom_call_target="InvertDiagBlocksLowerTriangular" | custom-call | tf_op jit(solution)/shard_map/jit(cholesky)/cholesky | solution.py:119
  56.9 11.7 %cholesky.215 = f32[128,128]{1,0:T(8,128)S(1)} custom-call(f32[128,128]{1,0:T(8,128)S(1)} %cholesky.267), custom_call_target="Cholesky" | custom-call | tf_op jit(solution)/shard_map/jit(cholesky)/cholesky | solution.py:119
  69.3 10.0 %custom-call.35 = f32[1,128,128]{1,2,0:T(8,128)S(1)} custom-call(f32[1,128,128]{2,1,0:T(8,128)S(1)} %get-tuple-element.52), custom_call_target="InvertDiagBlocksLowerTriangular" | custom-call | tf_op jit(solution)/shard_map/jit(cholesky)/cholesky | solution.py:119
  79.6 1.3 convolution_subtract_fusion.1
  80.9 11.7 %cholesky.236 = f32[128,128]{1,0:T(8,128)S(1)} custom-call(f32[128,128]{1,0:T(8,128)S(1)} %cholesky.272), custom_call_target="Cholesky" | custom-call | tf_op jit(solution)/shard_map/jit(cholesky)/cholesky | solution.py:119
  93.3 9.8 %custom-call.36 = f32[1,128,128]{1,2,0:T(8,128)S(1)} custom-call(f32[1,128,128]{2,1,0:T(8,128)S(1)} %get-tuple-element.49), custom_call_target="InvertDiagBlocksLowerTriangular" | custom-call | tf_op jit(solution)/shard_map/jit(cholesky)/cholesky | solution.py:119
  104.6 12.1 %cholesky.253 = f32[128,128]{1,0:T(8,128)S(1)} custom-call(f32[128,128]{1,0:T(8,128)S(1)} %convolution_subtract_fusion.2), custom_call_target="Cholesky" | custom-call | tf_op jit(solution)/shard_map/jit(cholesky)/cholesky | solution.py:119
  119.9 10.7 %while.1 = (s32[]{:T(128)}, f32[512,512]{1,0:T(8,128)S(1)}, s32[4,2]{0,1:T(2,128)S(1)}, f32[4,128,128]{2,1,0:T(8,128)}, s32[]{:T(128)}) while((s32[]{:T(128)}, f32[512,512]{1,0:T(8,128)S(1)}, s32[4,2]{0,1:T(2,128)S(1)}, f32[4,128,128]{2,1,0:T(8,128)}, s32[]{:T(128)}) %tuple.59), condition=%wide.while_cond, body=%wide.while_body.sunk | while | flops 2 | bytes 132205 | solution.py:100
  120.6 2.0 bitcast_dynamic-update-slice_fusion.2
  123.3 2.0 bitcast_dynamic-update-slice_fusion.2
  125.9 2.0 bitcast_dynamic-update-slice_fusion.2
  128.6 2.0 bitcast_dynamic-update-slice_fusion.2
  131.3 9.1 %collective-permute-start.3 = (f32[34,1,16]{0,2,1:T(8,128)S(1)}, f32[34,1,16]{0,2,1:T(8,128)S(1)}, u32[]{:S(2)}, u32[]{:S(2)}) collective-permute-start(f32[34,1,16]{0,2,1:T(8,128)S(1)} %get-tuple-element.62), channel_id=1, source_target_pairs={{0,8},{8,16},{16,24},{1,9},{9,17},{17,25},{2,10},{10,18},{18,26},{... | collective-permute-start | bytes 6536 | tf_op jit(solution)/shard_map/ppermute | solution.py:17
  140.4 1.3 collective-permute-start.2
  141.8 9.4 %collective-permute-done.2 = f32[34,1,16]{0,2,1:T(8,128)S(1)} collective-permute-done((f32[34,1,16]{0,2,1:T(8,128)S(1)}, f32[34,1,16]{0,2,1:T(8,128)S(1)}, u32[]{:S(2)}, u32[]{:S(2)}) %collective-permute-start.2) | collective-permute-done | bytes 2208 | tf_op jit(solution)/shard_map/ppermute | solution.py:19
  151.2 2.0 collective-permute-start.4
  153.2 2.3 collective-permute-start.5
  155.6 40.8 %custom-call.37 = f32[4,128,128]{1,2,0:T(8,128)} custom-call(f32[4,128,128]{2,1,0:T(8,128)} %get-tuple-element.9), custom_call_target="InvertDiagBlocksLowerTriangular" | custom-call | tf_op jit(solution)/shard_map/jit(_cho_solve)/triangular_solve | solution.py:100
  198.8 8.8 %all-to-all-start = ((f32[16,1,3072]{2,1,0:T(1,128)}), f32[16,1,3072]{2,1,0:T(1,128)S(1)}, u32[]{:S(2)}, u32[]{:S(2)}) async-start(f32[16,1,3072]{2,1,0:T(1,128)} %reshape.299), calls=%async_computation | async-start | bytes 393216 | tf_op jit(solution)/shard_map/all_to_all | solution.py:34
  208.9 6.9 %all-to-all-done = f32[16,1,3072]{2,1,0:T(1,128)S(1)} async-done(((f32[16,1,3072]{2,1,0:T(1,128)}), f32[16,1,3072]{2,1,0:T(1,128)S(1)}, u32[]{:S(2)}, u32[]{:S(2)}) %all-to-all-start) | async-done | bytes 196640 | tf_op jit(solution)/shard_map/all_to_all | solution.py:34
  218.6 1.3 bitcast_bitcast_fusion
  219.9 1.4 copy.114
  221.2 2.1 reshape.274
  228.1 2.3 collective-permute-start.12
  230.4 6.2 %collective-permute-start.13 = (f32[3,1,2,16]{1,3,2,0:T(8,128)S(1)}, f32[3,1,2,16]{1,3,2,0:T(8,128)S(1)}, u32[]{:S(2)}, u32[]{:S(2)}) collective-permute-start(f32[3,1,2,16]{1,3,2,0:T(8,128)S(1)} %get-tuple-element.61), channel_id=1, source_target_pairs={{32,0},{64,32},{96,64},{128,96},{160,128},{192,160},{224,192},{256... | collective-permute-start | bytes 1160 | tf_op jit(solution)/shard_map/ppermute | solution.py:19
  238.5 7.8 %collective-permute-start.14 = (f32[3,34,1,16]{1,3,2,0:T(8,128)S(1)}, f32[3,34,1,16]{1,3,2,0:T(8,128)S(1)}, u32[]{:S(2)}, u32[]{:S(2)}) collective-permute-start(f32[3,34,1,16]{1,3,2,0:T(8,128)S(1)} %get-tuple-element.58), channel_id=1, source_target_pairs={{0,8},{8,16},{16,24},{1,9},{9,17},{17,25},{2,10},{10,18},{18,26},{... | collective-permute-start | bytes 19592 | tf_op jit(solution)/shard_map/ppermute | solution.py:17
  246.2 1.3 collective-permute-start.15
  248.1 6.9 %collective-permute-start.9 = (bf16[1,16,128]{2,0,1:T(2,128)(2,1)S(1)}, bf16[1,16,128]{2,0,1:T(2,128)(2,1)S(1)}, u32[]{:S(2)}, u32[]{:S(2)}) collective-permute-start(bf16[1,16,128]{2,0,1:T(2,128)(2,1)S(1)} %copy-done.11), channel_id=1, source_target_pairs={{32,0},{64,32},{96,64},{128,96},{160,128},{192,160},{224,192},{256... | collective-permute-start | bytes 12296 | tf_op jit(solution)/shard_map/ppermute | solution.py:50
  256.3 8.5 %collective-permute-start.7 = (bf16[256,1,128]{2,0,1:T(8,128)(2,1)}, bf16[256,1,128]{2,0,1:T(8,128)(2,1)S(1)}, u32[]{:S(2)}, u32[]{:S(2)}) collective-permute-start(bf16[256,1,128]{2,0,1:T(8,128)(2,1)} %get-tuple-element.38), channel_id=1, source_target_pairs={{0,8},{8,16},{16,24},{1,9},{9,17},{17,25},{2,10},{10,18},{18,26},{... | collective-permute-start | bytes 196616 | tf_op jit(solution)/shard_map/ppermute | solution.py:49
  264.7 2.1 copy.125
  266.8 1.3 collective-permute-start.10
  268.2 1.9 collective-permute-start.16
  270.3 3.6 %collective-permute-start.17 = (f32[3,34,4,1]{1,3,2,0:T(1,128)S(1)}, f32[3,34,4,1]{1,3,2,0:T(1,128)S(1)}, u32[]{:S(2)}, u32[]{:S(2)}) collective-permute-start(f32[3,34,4,1]{1,3,2,0:T(1,128)S(1)} %get-tuple-element.41), channel_id=1, source_target_pairs={{1,0},{2,1},{3,2},{4,3},{5,4},{6,5},{7,6},{9,8},{10,9},{11,10},{12... | collective-permute-start | bytes 4904 | tf_op jit(solution)/shard_map/ppermute | solution.py:19
  274.0 3.5 %collective-permute-done.10 = bf16[256,1,128]{2,0,1:T(8,128)(2,1)S(1)} collective-permute-done((bf16[256,1,128]{2,0,1:T(8,128)(2,1)}, bf16[256,1,128]{2,0,1:T(8,128)(2,1)S(1)}, u32[]{:S(2)}, u32[]{:S(2)}) %collective-permute-start.10) | collective-permute-done | bytes 65568 | tf_op jit(solution)/shard_map/ppermute | solution.py:50
  277.5 6.0 %fusion.11 = f32[258,18,130]{2,0,1:T(8,128)S(1)} fusion(bf16[256,16,1]{2,0,1:T(8,128)(2,1)} %copy.125, bf16[256,1,128]{2,0,1:T(8,128)(2,1)S(1)} %collective-permute-done.10, bf16[256,1,128]{2,0,1:T(8,128)(2,1)S(1)} %collective-permute-done.7, bf16[256,16,1]{2,0,1:T(8,128)(2,1)S(1)} %copy.118, bf16[1,16,128]{2,0,1:T(2,128)(2,1)S(1)} %collective-permute-done.9, ...), kind=kLoop, calls=%fused_computation.21 | loop fusion | flops 18111600 | bytes 3619104 | tf_op jit(solution)/shard_map/convert_element_type | solution.py:132
  285.0 10.0 %fusion.25 = f32[3,256,16,128]{3,1,2,0:T(8,128)S(1)} fusion(f32[3,256,16,18]{1,2,3,0:T(8,128)S(1)} %convolution_bitcast_fusion.2, f32[128]{0:T(128)S(1)} %copy-done.21, s32[128]{0:T(128)S(1)} %copy-done.13, f32[128]{0:T(128)S(1)} %get-tuple-element.72, s32[128]{0:T(128)S(1)} %copy-done.16, f32[128]{0:T(128)S(1)} %get-tuple-element.73, ...), kind=kOutput, calls=%fused_computation.48 | convolution fusion | flops 339761664 | bytes 7179520 | tf_op jit(solution)/shard_map/nijc,kc->nijk/dot_general | solution.py:130
  295.1 4.5 %fusion.17 = bf16[256,16,128]{2,0,1:T(8,128)(2,1)S(1)} fusion(f32[3,256,16,128]{3,1,2,0:T(8,128)S(1)} %fusion.25, f32[258,18,130]{2,0,1:T(8,128)S(1)} %fusion.11, bf16[256,16,128]{2,1,0:T(8,128)(2,1)S(1)} %copy-done.6, bf16[256,16,128]{2,1,0:T(8,128)(2,1)S(1)} %copy-done), kind=kLoop, calls=%fused_computation.28 | loop fusion | flops 8388608 | bytes 22020096 | tf_op jit(solution)/shard_map/convert_element_type | solution.py:135
  299.6 1.6 copy.128
  (167 shorter events, 36.9 us)
Async XLA Ops:
  2.1 4.5 %copy-start.1 = (bf16[256,16,128]{2,0,1:T(8,128)(2,1)}, bf16[256,16,128]{2,0,1:T(8,128)(2,1)S(1)}, u32[]{:S(2)}) copy-start(bf16[256,16,128]{2,0,1:T(8,128)(2,1)S(1)} %copy.116) | copy-start | bytes 3145732
  2.8 267.4 %collective-permute-start.8 = (bf16[1,16,128]{2,0,1:T(2,128)(2,1)}, bf16[1,16,128]{2,0,1:T(2,128)(2,1)}, u32[]{:S(2)}, u32[]{:S(2)}) collective-permute-start(bf16[1,16,128]{2,0,1:T(2,128)(2,1)} %get-tuple-element.34), channel_id=1, source_target_pairs={{0,32},{32,64},{64,96},{96,128},{128,160},{160,192},{192,224},{224... | collective-permute-start | bytes 12296 | tf_op jit(solution)/shard_map/ppermute | solution.py:49
  6.6 0.5 copy-start.12
  8.9 7.7 %copy-start = (bf16[256,16,128]{2,1,0:T(8,128)(2,1)S(1)}, bf16[256,16,128]{2,1,0:T(8,128)(2,1)}, u32[]{:S(2)}) copy-start(bf16[256,16,128]{2,1,0:T(8,128)(2,1)} %param.3) | copy-start | bytes 3145732
  9.9 121.3 %collective-permute-start = (f32[1,2,16]{0,2,1:T(8,128)S(1)}, f32[1,2,16]{0,2,1:T(8,128)S(1)}, u32[]{:S(2)}, u32[]{:S(2)}) collective-permute-start(f32[1,2,16]{0,2,1:T(8,128)S(1)} %get-tuple-element.64), channel_id=1, source_target_pairs={{32,0},{64,32},{96,64},{128,96},{160,128},{192,160},{224,192},{256... | collective-permute-start | bytes 392 | tf_op jit(solution)/shard_map/ppermute | solution.py:19
  14.6 116.6 %collective-permute-start.1 = (f32[1,2,16]{0,2,1:T(8,128)S(1)}, f32[1,2,16]{0,2,1:T(8,128)S(1)}, u32[]{:S(2)}, u32[]{:S(2)}) collective-permute-start(f32[1,2,16]{0,2,1:T(8,128)S(1)} %get-tuple-element.65), channel_id=1, source_target_pairs={{0,32},{32,64},{64,96},{96,128},{128,160},{160,192},{192,224},{224... | collective-permute-start | bytes 392 | tf_op jit(solution)/shard_map/ppermute | solution.py:17
  18.5 237.7 %collective-permute-start.11 = (bf16[256,16,1]{0,1,2:T(8,128)(2,1)}, bf16[256,16,1]{0,1,2:T(8,128)(2,1)}, u32[]{:S(2)}, u32[]{:S(2)}) collective-permute-start(bf16[256,16,1]{0,1,2:T(8,128)(2,1)} %copy.133), channel_id=1, source_target_pairs={{1,0},{2,1},{3,2},{4,3},{5,4},{6,5},{7,6},{9,8},{10,9},{11,10},{12... | collective-permute-start | bytes 24584 | tf_op jit(solution)/shard_map/ppermute | solution.py:50
  22.0 20.3 %copy-start.5 = (bf16[256,16,128]{2,1,0:T(8,128)(2,1)S(1)}, bf16[256,16,128]{2,1,0:T(8,128)(2,1)}, u32[]{:S(2)}) copy-start(bf16[256,16,128]{2,1,0:T(8,128)(2,1)} %param.4) | copy-start | bytes 3145732
  22.0 226.2 %collective-permute-start.6 = (bf16[256,16,1]{0,1,2:T(8,128)(2,1)}, bf16[256,16,1]{0,1,2:T(8,128)(2,1)}, u32[]{:S(2)}, u32[]{:S(2)}) collective-permute-start(bf16[256,16,1]{0,1,2:T(8,128)(2,1)} %copy.132), channel_id=1, source_target_pairs={{0,1},{1,2},{2,3},{3,4},{4,5},{5,6},{6,7},{8,9},{9,10},{10,11},{11... | collective-permute-start | bytes 24584 | tf_op jit(solution)/shard_map/ppermute | solution.py:49
  28.8 1.0 copy-start.7
  55.6 64.3 %copy-start.23 = (s32[4]{0:T(128)S(1)}, s32[4]{0:T(128)}, u32[]{:S(2)}) copy-start(s32[4]{0:T(128)} %iota_multiply_fusion) | copy-start | bytes 52
  130.7 24.9 %copy-start.3 = (f32[512,512]{1,0:T(8,128)}, f32[512,512]{1,0:T(8,128)S(1)}, u32[]{:S(2)}) copy-start(f32[512,512]{1,0:T(8,128)S(1)} %get-tuple-element.132) | copy-start | bytes 3145732
  130.7 66.6 %copy-start.10 = (f32[3,32,2,16]{1,3,2,0:T(8,128)S(1)}, f32[3,32,2,16]{1,3,2,0:T(8,128)}, u32[]{:S(2)}) copy-start(f32[3,32,2,16]{1,3,2,0:T(8,128)} %param.5) | copy-start | bytes 36868
  131.3 10.4 %collective-permute-start.3 = (f32[34,1,16]{0,2,1:T(8,128)S(1)}, f32[34,1,16]{0,2,1:T(8,128)S(1)}, u32[]{:S(2)}, u32[]{:S(2)}) collective-permute-start(f32[34,1,16]{0,2,1:T(8,128)S(1)} %get-tuple-element.62), channel_id=1, source_target_pairs={{0,8},{8,16},{16,24},{1,9},{9,17},{17,25},{2,10},{10,18},{18,26},{... | collective-permute-start | bytes 6536 | tf_op jit(solution)/shard_map/ppermute | solution.py:17
  140.4 10.7 %collective-permute-start.2 = (f32[34,1,16]{0,2,1:T(8,128)S(1)}, f32[34,1,16]{0,2,1:T(8,128)S(1)}, u32[]{:S(2)}, u32[]{:S(2)}) collective-permute-start(f32[34,1,16]{0,2,1:T(8,128)S(1)} %get-tuple-element.63), channel_id=1, source_target_pairs={{8,0},{16,8},{24,16},{9,1},{17,9},{25,17},{10,2},{18,10},{26,18},{... | collective-permute-start | bytes 6536 | tf_op jit(solution)/shard_map/ppermute | solution.py:19
  151.2 46.1 %collective-permute-start.4 = (f32[34,4,1]{0,2,1:T(1,128)S(1)}, f32[34,4,1]{0,2,1:T(1,128)S(1)}, u32[]{:S(2)}, u32[]{:S(2)}) collective-permute-start(f32[34,4,1]{0,2,1:T(1,128)S(1)} %get-tuple-element.56), channel_id=1, source_target_pairs={{1,0},{2,1},{3,2},{4,3},{5,4},{6,5},{7,6},{9,8},{10,9},{11,10},{12... | collective-permute-start | bytes 1640 | tf_op jit(solution)/shard_map/ppermute | solution.py:19
  153.2 44.1 %collective-permute-start.5 = (f32[34,4,1]{0,2,1:T(1,128)S(1)}, f32[34,4,1]{0,2,1:T(1,128)S(1)}, u32[]{:S(2)}, u32[]{:S(2)}) collective-permute-start(f32[34,4,1]{0,2,1:T(1,128)S(1)} %get-tuple-element.57), channel_id=1, source_target_pairs={{0,1},{1,2},{2,3},{3,4},{4,5},{5,6},{6,7},{8,9},{9,10},{10,11},{11... | collective-permute-start | bytes 1640 | tf_op jit(solution)/shard_map/ppermute | solution.py:17
  197.2 11.0 %copy-start.2 = (bf16[256,16,128]{2,0,1:T(8,128)(2,1)S(1)}, bf16[256,16,128]{2,0,1:T(8,128)(2,1)}, u32[]{:S(2)}) copy-start(bf16[256,16,128]{2,0,1:T(8,128)(2,1)} %copy-done.1) | copy-start | bytes 3145732
  198.8 17.0 %all-to-all-start = ((f32[16,1,3072]{2,1,0:T(1,128)}), f32[16,1,3072]{2,1,0:T(1,128)S(1)}, u32[]{:S(2)}, u32[]{:S(2)}) async-start(f32[16,1,3072]{2,1,0:T(1,128)} %reshape.299), calls=%async_computation | async-start | bytes 393216 | tf_op jit(solution)/shard_map/all_to_all | solution.py:34
  218.6 5.7 %copy-start.9 = (f32[4,128,128]{1,2,0:T(8,128)S(1)}, f32[4,128,128]{1,2,0:T(8,128)}, u32[]{:S(2)}) copy-start(f32[4,128,128]{1,2,0:T(8,128)} %custom-call.37) | copy-start | bytes 786436
  218.6 5.9 %copy-start.4 = (f32[512,512]{1,0:T(8,128)S(1)}, f32[512,512]{1,0:T(8,128)}, u32[]{:S(2)}) copy-start(f32[512,512]{1,0:T(8,128)} %copy-done.3) | copy-start | bytes 3145732
  223.4 24.8 %copy-start.11 = (bf16[1,16,128]{2,0,1:T(2,128)(2,1)S(1)}, bf16[1,16,128]{2,0,1:T(2,128)(2,1)}, u32[]{:S(2)}) copy-start(bf16[1,16,128]{2,0,1:T(2,128)(2,1)} %get-tuple-element.35) | copy-start | bytes 12292
  228.0 55.5 %copy-start.8 = (f32[3,32,2,16]{1,3,2,0:T(8,128)}, f32[3,32,2,16]{1,3,2,0:T(8,128)S(1)}, u32[]{:S(2)}) copy-start(f32[3,32,2,16]{1,3,2,0:T(8,128)S(1)} %add.453) | copy-start | bytes 36868
  228.1 9.1 %collective-permute-start.12 = (f32[3,1,2,16]{1,3,2,0:T(8,128)S(1)}, f32[3,1,2,16]{1,3,2,0:T(8,128)S(1)}, u32[]{:S(2)}, u32[]{:S(2)}) collective-permute-start(f32[3,1,2,16]{1,3,2,0:T(8,128)S(1)} %get-tuple-element.60), channel_id=1, source_target_pairs={{0,32},{32,64},{64,96},{96,128},{128,160},{160,192},{192,224},{224... | collective-permute-start | bytes 1160 | tf_op jit(solution)/shard_map/ppermute | solution.py:17
  230.4 7.9 %collective-permute-start.13 = (f32[3,1,2,16]{1,3,2,0:T(8,128)S(1)}, f32[3,1,2,16]{1,3,2,0:T(8,128)S(1)}, u32[]{:S(2)}, u32[]{:S(2)}) collective-permute-start(f32[3,1,2,16]{1,3,2,0:T(8,128)S(1)} %get-tuple-element.61), channel_id=1, source_target_pairs={{32,0},{64,32},{96,64},{128,96},{160,128},{192,160},{224,192},{256... | collective-permute-start | bytes 1160 | tf_op jit(solution)/shard_map/ppermute | solution.py:19
  238.5 28.4 %collective-permute-start.14 = (f32[3,34,1,16]{1,3,2,0:T(8,128)S(1)}, f32[3,34,1,16]{1,3,2,0:T(8,128)S(1)}, u32[]{:S(2)}, u32[]{:S(2)}) collective-permute-start(f32[3,34,1,16]{1,3,2,0:T(8,128)S(1)} %get-tuple-element.58), channel_id=1, source_target_pairs={{0,8},{8,16},{16,24},{1,9},{9,17},{17,25},{2,10},{10,18},{18,26},{... | collective-permute-start | bytes 19592 | tf_op jit(solution)/shard_map/ppermute | solution.py:17
  246.2 21.9 %collective-permute-start.15 = (f32[3,34,1,16]{1,3,2,0:T(8,128)S(1)}, f32[3,34,1,16]{1,3,2,0:T(8,128)S(1)}, u32[]{:S(2)}, u32[]{:S(2)}) collective-permute-start(f32[3,34,1,16]{1,3,2,0:T(8,128)S(1)} %get-tuple-element.59), channel_id=1, source_target_pairs={{8,0},{16,8},{24,16},{9,1},{17,9},{25,17},{10,2},{18,10},{26,18},{... | collective-permute-start | bytes 19592 | tf_op jit(solution)/shard_map/ppermute | solution.py:19
  248.1 25.8 %collective-permute-start.9 = (bf16[1,16,128]{2,0,1:T(2,128)(2,1)S(1)}, bf16[1,16,128]{2,0,1:T(2,128)(2,1)S(1)}, u32[]{:S(2)}, u32[]{:S(2)}) collective-permute-start(bf16[1,16,128]{2,0,1:T(2,128)(2,1)S(1)} %copy-done.11), channel_id=1, source_target_pairs={{32,0},{64,32},{96,64},{128,96},{160,128},{192,160},{224,192},{256... | collective-permute-start | bytes 12296 | tf_op jit(solution)/shard_map/ppermute | solution.py:50
  256.3 17.7 %collective-permute-start.7 = (bf16[256,1,128]{2,0,1:T(8,128)(2,1)}, bf16[256,1,128]{2,0,1:T(8,128)(2,1)S(1)}, u32[]{:S(2)}, u32[]{:S(2)}) collective-permute-start(bf16[256,1,128]{2,0,1:T(8,128)(2,1)} %get-tuple-element.38), channel_id=1, source_target_pairs={{0,8},{8,16},{16,24},{1,9},{9,17},{17,25},{2,10},{10,18},{18,26},{... | collective-permute-start | bytes 196616 | tf_op jit(solution)/shard_map/ppermute | solution.py:49
  266.8 10.7 %collective-permute-start.10 = (bf16[256,1,128]{2,0,1:T(8,128)(2,1)}, bf16[256,1,128]{2,0,1:T(8,128)(2,1)S(1)}, u32[]{:S(2)}, u32[]{:S(2)}) collective-permute-start(bf16[256,1,128]{2,0,1:T(8,128)(2,1)} %get-tuple-element.39), channel_id=1, source_target_pairs={{8,0},{16,8},{24,16},{9,1},{17,9},{25,17},{10,2},{18,10},{26,18},{... | collective-permute-start | bytes 196616 | tf_op jit(solution)/shard_map/ppermute | solution.py:50
  268.2 15.3 %collective-permute-start.16 = (f32[3,34,4,1]{1,3,2,0:T(1,128)S(1)}, f32[3,34,4,1]{1,3,2,0:T(1,128)S(1)}, u32[]{:S(2)}, u32[]{:S(2)}) collective-permute-start(f32[3,34,4,1]{1,3,2,0:T(1,128)S(1)} %get-tuple-element.40), channel_id=1, source_target_pairs={{0,1},{1,2},{2,3},{3,4},{4,5},{5,6},{6,7},{8,9},{9,10},{10,11},{11... | collective-permute-start | bytes 4904 | tf_op jit(solution)/shard_map/ppermute | solution.py:17
  270.2 13.4 %copy-start.24 = (s32[256]{0:T(256)S(1)}, s32[256]{0:T(256)}, u32[]{:S(2)}) copy-start(s32[256]{0:T(256)} %broadcast_add_fusion.1) | copy-start | bytes 3076
  270.2 13.4 %copy-start.25 = (f32[256]{0:T(256)S(1)}, f32[256]{0:T(256)}, u32[]{:S(2)}) copy-start(f32[256]{0:T(256)} %fusion.167) | copy-start | bytes 3076
  270.2 13.4 %copy-start.26 = (pred[256]{0:T(512)(128)(4,1)S(1)}, pred[256]{0:T(512)(128)(4,1)}, u32[]{:S(2)}) copy-start(pred[256]{0:T(512)(128)(4,1)} %get-tuple-element.86) | copy-start | bytes 772
  270.2 13.4 %copy-start.27 = (pred[256]{0:T(512)(128)(4,1)S(1)}, pred[256]{0:T(512)(128)(4,1)}, u32[]{:S(2)}) copy-start(pred[256]{0:T(512)(128)(4,1)} %get-tuple-element.87) | copy-start | bytes 772
  270.2 13.8 %copy-start.18 = (pred[16]{0:T(512)(128)(4,1)S(1)}, pred[16]{0:T(512)(128)(4,1)}, u32[]{:S(2)}) copy-start(pred[16]{0:T(512)(128)(4,1)} %get-tuple-element.78) | copy-start | bytes 52
  270.2 13.8 %copy-start.19 = (pred[16]{0:T(512)(128)(4,1)S(1)}, pred[16]{0:T(512)(128)(4,1)}, u32[]{:S(2)}) copy-start(pred[16]{0:T(512)(128)(4,1)} %get-tuple-element.79) | copy-start | bytes 52
  270.2 13.8 %copy-start.20 = (s32[16]{0:T(128)S(1)}, s32[16]{0:T(128)}, u32[]{:S(2)}) copy-start(s32[16]{0:T(128)} %get-tuple-element.69) | copy-start | bytes 196
  270.2 13.8 %copy-start.22 = (s32[16]{0:T(128)S(1)}, s32[16]{0:T(128)}, u32[]{:S(2)}) copy-start(s32[16]{0:T(128)} %broadcast_add_fusion.4) | copy-start | bytes 196
  270.3 14.7 %copy-start.13 = (s32[128]{0:T(128)S(1)}, s32[128]{0:T(128)}, u32[]{:S(2)}) copy-start(s32[128]{0:T(128)} %copy-done.12) | copy-start | bytes 1540
  270.3 14.7 %copy-start.14 = (pred[128]{0:T(512)(128)(4,1)S(1)}, pred[128]{0:T(512)(128)(4,1)}, u32[]{:S(2)}) copy-start(pred[128]{0:T(512)(128)(4,1)} %get-tuple-element.76) | copy-start | bytes 388
  270.3 14.7 %copy-start.15 = (pred[128]{0:T(512)(128)(4,1)S(1)}, pred[128]{0:T(512)(128)(4,1)}, u32[]{:S(2)}) copy-start(pred[128]{0:T(512)(128)(4,1)} %get-tuple-element.77) | copy-start | bytes 388
  270.3 14.7 %copy-start.16 = (s32[128]{0:T(128)S(1)}, s32[128]{0:T(128)}, u32[]{:S(2)}) copy-start(s32[128]{0:T(128)} %get-tuple-element.74) | copy-start | bytes 1540
  270.3 14.7 %copy-start.17 = (s32[128]{0:T(128)S(1)}, s32[128]{0:T(128)}, u32[]{:S(2)}) copy-start(s32[128]{0:T(128)} %get-tuple-element.75) | copy-start | bytes 1540
  270.3 14.7 %copy-start.21 = (f32[128]{0:T(128)S(1)}, f32[128]{0:T(128)}, u32[]{:S(2)}) copy-start(f32[128]{0:T(128)} %fusion.169) | copy-start | bytes 1540
  270.3 13.2 %collective-permute-start.17 = (f32[3,34,4,1]{1,3,2,0:T(1,128)S(1)}, f32[3,34,4,1]{1,3,2,0:T(1,128)S(1)}, u32[]{:S(2)}, u32[]{:S(2)}) collective-permute-start(f32[3,34,4,1]{1,3,2,0:T(1,128)S(1)} %get-tuple-element.41), channel_id=1, source_target_pairs={{1,0},{2,1},{3,2},{4,3},{5,4},{6,5},{7,6},{9,8},{10,9},{11,10},{12... | collective-permute-start | bytes 4904 | tf_op jit(solution)/shard_map/ppermute | solution.py:19
  285.0 10.0 %copy-start.6 = (bf16[256,16,128]{2,1,0:T(8,128)(2,1)S(1)}, bf16[256,16,128]{2,1,0:T(8,128)(2,1)}, u32[]{:S(2)}) copy-start(bf16[256,16,128]{2,1,0:T(8,128)(2,1)} %param.4) | copy-start | bytes 3145732
where the time goes:
time: 306 us; the launch traced here: 301 us
  other arithmetic  141 us (46%)
  starting transfers between devices  78.4 us (26%)
  local copies, waits for them, and re-layouts  33.8 us (11%)
  matrix products  23.1 us (8%)
  waiting for transfers between devices  21 us (7%)
  between operations  4.24 us (1%)
    another operation x15, other arithmetic, on_device(): factor = jnp.linalg.cholesky(line_matrix(lines))  80.7 us
    another operation x4, other arithmetic, line_solve(): solved = jax.scipy.linalg.cho_solve((factor, True), flat)  41.5 us
    ppermute x6, starting transfers between devices, padded_2(): lax.ppermute(tail, axis, [(i, (i + 1) % count) for i in range(ends)])  25.4 us
    ppermute x6, starting transfers between devices, padded_2(): lax.ppermute(head, axis, [((i + 1) % count, i) for i in range(ends)])  19.1 us
    ppermute x3, starting transfers between devices, extended(): lax.ppermute(last, axis, up)  15 us
    another operation x13, local copies, waits for them, and re-layouts  10.8 us
    ppermute x6, waiting for transfers between devices, padded_2(): lax.ppermute(head, axis, [((i + 1) % count, i) for i in range(ends)])  10.5 us
    ppermute x3, starting transfers between devices, extended(): lax.ppermute(initial, axis, [(b, a) for a, b in up])  10.1 us
  transfers between devices with their start and end apart: 19, of which 4 were waited for; matrix products, arithmetic and copies ran while one was open for 59% of the time, Pallas kernels for 0%

commit v1 on v0

v1 whole, which is shorter than its diff:
```python
import numpy as np
import jax
import jax.numpy as jnp
from jax import lax
from jax.experimental import pallas as pl
from jax.experimental.pallas import tpu as pltpu
from jax.sharding import PartitionSpec as P

STIFFNESS = 64.0
SPAN = 20
VMEM = pl.BlockSpec(memory_space=pltpu.VMEM)
HIGHEST = lax.Precision.HIGHEST
F32 = jnp.float32
BF16 = jnp.bfloat16
SLAB = 40
EXT = 40


def inverse_entry(lines):
    diagonal = 1.0 + 2.0 * STIFFNESS
    root = (diagonal - np.sqrt(diagonal**2 - 4.0 * STIFFNESS**2)) / (2.0 * STIFFNESS)
    theta = -np.log(root)
    scale = 1.0 / (2.0 * STIFFNESS * np.sinh(theta) * (1.0 - root ** (2.0 * (lines + 1))))

    def first(i):
        return 1.0 - root ** (2.0 * (i + 1))

    def last(i):
        return 1.0 - root ** (2.0 * (lines - i))

    return root, scale, first, last


def solve_tables(devices, cells):
    lines = devices * cells
    root, scale, first, last = inverse_entry(lines)
    local = np.arange(cells)
    weights = np.zeros((devices, 8, cells))
    table = np.zeros((devices, EXT, cells + 4 * devices))
    everyone = np.arange(devices)
    for p in range(devices):
        at = p * cells + local
        weights[p, 0] = first(at) * root ** (cells - 1.0 - local)
        weights[p, 1] = last(at) * root**local
        rows = np.concatenate([at, [p * cells - 1, p * cells + cells]])[:, None]
        used = slice(0, cells + 2)

        def entry(columns):
            low, high = np.minimum(rows, columns), np.maximum(rows, columns)
            return scale * root ** (1.0 * (high - low)) * first(low) * last(high)

        table[p, used, :cells] = entry(at[None, :])
        below = (everyone < p)[None, :]
        gap = np.where(below, rows - (everyone * cells + cells - 1)[None, :], 0)
        table[p, used, cells : cells + devices] = below * scale * last(rows) * root ** (1.0 * gap)
        above = (everyone > p)[None, :]
        gap = np.where(above, (everyone * cells)[None, :] - rows, 0)
        table[p, used, cells + devices : cells + 2 * devices] = (
            above * scale * first(rows) * root ** (1.0 * gap)
        )
        table[p, used, cells + 2 * devices : cells + 3 * devices] = entry(
            (everyone * cells)[None, :]
        )
        table[p, used, cells + 3 * devices :] = entry((everyone * cells + cells - 1)[None, :])
    return weights.astype(np.float32), table.astype(np.float32)


def iota(shape, dim):
    return lax.broadcasted_iota(jnp.int32, shape, dim)


def roll(value, shift, axis):
    size = value.shape[axis]
    return pltpu.roll(value, shift % size, axis)


def exact_dot(a, b, dims):
    return lax.dot_general(a, b, (dims, ((), ())), precision=HIGHEST, preferred_element_type=F32)


def put_split(ref, start, value):
    rows = value.shape[0]
    for part in range(3):
        piece = value.astype(BF16)
        ref[pl.ds(start + part * rows, rows), :] = piece
        value = value - piece.astype(F32)


def get_split(ref, rows):
    return (
        ref[0:rows, :].astype(F32)
        + ref[rows : 2 * rows, :].astype(F32)
        + ref[2 * rows : 3 * rows, :].astype(F32)
    )


def bin_kernel(
    chunk, ref_ref, def_ref, disp_ref,
    coarse_ref, up_ref, down_ref, y_high_ref, y_low_ref,
    bins, faces,
):
    step = pl.program_id(0)
    cells = chunk // 8
    row0 = pl.multiple_of(step * cells, cells)
    for k, image in enumerate((ref_ref, def_ref)):
        for c in range(cells):
            planes = image[pl.ds(c * 8, 8)].astype(F32)
            total = planes.sum(0)
            for y in range(2):
                bins[k, y, pl.ds(row0 + c, 1), :] = total[y * 8 : y * 8 + 8].sum(
                    0, keepdims=True
                )
    flat = ref_ref[...].reshape(chunk * 16, 128)
    lane = iota((16, 128), 1)
    row = iota((16, 128), 0)
    pick = jnp.where(
        ((row == 0) & (lane == 127)) | ((row == 1) & (lane == 0)), 1.0, 0.0
    ).astype(BF16)
    sides = lax.dot_general(
        pick, flat, (((1,), (1,)), ((), ())), preferred_element_type=F32
    )
    for c in range(cells):
        faces[0, pl.ds(row0 + c, 1), :] = sides[0:1, c * 128 : (c + 1) * 128]
        faces[1, pl.ds(row0 + c, 1), :] = sides[1:2, c * 128 : (c + 1) * 128]
    wide = ref_ref[...].astype(F32)
    x0 = pl.multiple_of(step * chunk, chunk)
    y_high_ref[pl.ds(x0, chunk), :] = wide[:, 15, :].astype(BF16)
    y_low_ref[pl.ds(x0, chunk), :] = wide[:, 0, :].astype(BF16)

    @pl.when(step == pl.num_programs(0) - 1)
    def _():
        rows = bins.shape[2]
        z = iota((128, 128), 0) // 8
        lanes = iota((128, 128), 1)
        place_lanes = iota((16, 128), 1)
        place_z = iota((16, 128), 0)
        whole = []
        for y in range(2):
            total = jnp.zeros((rows, 128), F32)
            for k in range(2):
                summer = jnp.where(lanes == k * SPAN + 2 + z, 1.0 / 32.0, 0.0)
                total += exact_dot(bins[k, y], summer, ((1,), (0,)))
            for k in range(3):
                place = jnp.where(place_lanes == (2 + k) * SPAN + 2 + place_z, 1.0, 0.0)
                total += exact_dot(disp_ref[k, y], place, ((0,), (0,)))
            coarse_ref[y] = total
            whole.append(total)
        position = iota((rows, 128), 1) % SPAN
        up = jnp.where(position < 2, roll(whole[0], -16, 1), roll(whole[1], -12, 1))
        down = jnp.where(position >= 18, roll(whole[0], 16, 1), roll(whole[1], 12, 1))
        put_split(up_ref, 0, up)
        put_split(down_ref, 0, down)
        up_ref[pl.ds(3 * rows, 32), :] = faces[0].astype(BF16)
        down_ref[pl.ds(3 * rows, 32), :] = faces[1].astype(BF16)


def z_kernel(
    devices, coarse_in, low_in, high_in, y_high_in, y_low_in, coarse_out, first_out, second_out
):
    rows = coarse_in.shape[1]
    me = lax.axis_index("gz")
    lane = iota((rows, 128), 1)
    position = lane % SPAN
    inside = lane < 5 * SPAN
    low = jnp.where(me > 0, get_split(low_in, rows), 0.0)
    high = jnp.where(me < devices - 1, get_split(high_in, rows), 0.0)
    whole = []
    for y in range(2):
        value = coarse_in[y]
        value = jnp.where((position < 2) & inside, roll(low, -4 * y, 1), value)
        value = jnp.where((position >= 18) & inside, roll(high, 4 * y, 1), value)
        coarse_out[y] = value
        whole.append(value)
    up = jnp.where(inside, whole[1], roll(whole[0], 100, 1))
    down = jnp.where(inside, whole[0], roll(whole[1], 100, 1))
    even = me % 2 == 0
    put_split(first_out, 0, jnp.where(even, up, down))
    put_split(second_out, 0, jnp.where(even, down, up))
    fine = y_high_in.shape[0]
    high_face, low_face = y_high_in[...], y_low_in[...]
    first_out[pl.ds(3 * rows, fine), :] = jnp.where(even, high_face, low_face)
    second_out[pl.ds(3 * rows, fine), :] = jnp.where(even, low_face, high_face)


def rhs_kernel(
    coarse_in, first_in, second_in, plane_low, plane_high, weights_in,
    slab_out, rhs_out, disp_out,
):
    rows = coarse_in.shape[1]
    devices = slab_out.shape[0]
    me = lax.axis_index("gx")
    even = lax.axis_index("gz") % 2 == 0
    first, second = get_split(first_in, rows), get_split(second_in, rows)
    below = jnp.where(even, first, second)
    above = jnp.where(even, second, first)
    layers = [below, coarse_in[0], coarse_in[1], above]
    lane = iota((rows, 128), 1)
    group = lane // 32
    position = lane % 32
    row = iota((rows, 128), 0)

    def packed(sources):
        value = jnp.zeros((rows, 128), F32)
        for y, (layer, at) in enumerate(sources):
            value = jnp.where(group == y, roll(layer, 32 * y - at, 1), value)
        return jnp.where(position < SPAN, value, 0.0)

    cell = packed([(layer, 0) for layer in layers])
    cell_below = packed([(below, 100), (layers[0], 0), (layers[1], 0), (layers[2], 0)])
    cell_above = packed([(layers[1], 0), (layers[2], 0), (layers[3], 0), (above, 100)])
    cell_def = packed([(layer, SPAN) for layer in layers])
    disp = [packed([(layer, (2 + k) * SPAN) for layer in layers]) for k in range(3)]
    slope_y = (cell_above - cell_below) * 0.5
    slope_z = (roll(cell, -1, 1) - roll(cell, 1, 1)) * 0.5
    slope_x = (roll(cell, -1, 0) - roll(cell, 1, 0)) * 0.5
    partial = cell_def - cell - (slope_y * disp[1] + slope_z * disp[2])
    mismatch = partial - slope_x * disp[0]
    keep = (position >= 1) & (position < SPAN - 1) & (row > 0) & (row < rows - 1)
    weights = weights_in[me]
    lines = []
    sums = []
    for k, slope in enumerate((slope_x, slope_y, slope_z)):
        rhs = jnp.where(keep, slope * mismatch, 0.0)
        rhs_out[k] = rhs
        disp_out[k] = disp[k]
        sums.append(exact_dot(weights, rhs, ((1,), (0,))))
    lines += [s[0:1] for s in sums] + [s[1:2] for s in sums]
    end = rows - 1
    lines += [cell[i : i + 1] for i in (0, 1, end - 1, end)]
    for value in (partial, slope_y, slope_z, disp[0]):
        lines += [value[0:1], value[end:]]
    lines += [disp[1][0:1], disp[2][0:1], disp[1][end:], disp[2][end:]]
    for i, line in enumerate(lines):
        for q in range(devices):
            slab_out[q, i : i + 1, :] = line
    low_plane = plane_low[0].astype(F32)
    high_plane = plane_high[0].astype(F32)
    blank = jnp.zeros((24 - len(lines), 128), F32)
    for q in range(devices):
        slab_out[q, len(lines) : 24, :] = blank
        slab_out[q, 24:40, :] = jnp.where(me > q, low_plane, high_plane)


def fine_kernel(
    chunk, slab_in, rhs_in, disp_in, table_in, z_low_in, z_high_in, first_in, second_in,
    ref_ref, before_ref, after_ref, def_ref,
    disp_out, out_ref,
    field, z_faces, y_faces,
):
    step = pl.program_id(0)
    devices = slab_in.shape[0]
    rows = rhs_in.shape[1]
    me = lax.axis_index("gx")
    me_z = lax.axis_index("gz")
    last_z = lax.axis_size("gz") - 1
    even = me_z % 2 == 0
    lower = jnp.maximum(me - 1, 0)
    upper = jnp.minimum(me + 1, devices - 1)

    @pl.when(step == 0)
    def _():
        lane = iota((devices, 128), 1)
        position = lane % 32
        q = iota((devices, 128), 0)
        keep = (position >= 1) & (position < SPAN - 1)

        def line(i):
            return slab_in[:, i, :]

        from_below = jnp.where(q > 0, roll(line(9), 1, 0), 0.0)
        from_above = jnp.where(q < devices - 1, roll(line(6), -1, 0), 0.0)
        slopes_0 = ((line(7) - from_below) * 0.5, line(12), line(14))
        slopes_1 = ((from_above - line(8)) * 0.5, line(13), line(15))
        mismatch_0 = line(10) - slopes_0[0] * line(16)
        mismatch_1 = line(11) - slopes_1[0] * line(17)
        own_lane = iota((16, 128), 1)
        own_z = iota((16, 128), 0)
        edge = iota((8, 128), 0)
        edge_lane = iota((8, 128), 1) % 32
        edge_keep = (edge_lane >= 1) & (edge_lane < SPAN - 1)
        solved = []
        for k in range(3):
            edge_0 = jnp.where(keep, slopes_0[k] * mismatch_0, 0.0)
            edge_1 = jnp.where(keep, slopes_1[k] * mismatch_1, 0.0)
            known = jnp.concatenate([rhs_in[k], line(k), line(3 + k), edge_0, edge_1], axis=0)
            moved = exact_dot(table_in[me], known, ((1,), (0,)))
            low_row = slab_in[lower, 17 if k == 0 else 19 + k : (17 if k == 0 else 19 + k) + 1, :]
            high_row = slab_in[upper, 16 if k == 0 else 17 + k : (16 if k == 0 else 17 + k) + 1, :]
            low_row = jnp.where(me > 0, low_row, 0.0)
            high_row = jnp.where(me < devices - 1, high_row, 0.0)
            outer = jnp.where(edge == 0, low_row, jnp.where(edge == 1, high_row, 0.0))
            inner = moved[:rows] + disp_in[k]
            outer = jnp.where(edge_keep, outer + moved[rows:], 0.0)
            for y in range(2):
                pick = jnp.where(own_lane == 32 * (y + 1) + 2 + own_z, 1.0, 0.0)
                disp_out[k, y] = exact_dot(pick, inner, ((1,), (1,)))
            inner_lane = iota((rows, 128), 1) % 32
            inner = jnp.where((inner_lane >= 1) & (inner_lane < SPAN - 1), inner, 0.0)
            solved += [inner, outer]
        whole = jnp.concatenate(solved, axis=0)
        parts = []
        for _ in range(3):
            piece = whole.astype(BF16)
            parts.append(piece)
            whole = whole - piece.astype(F32)
        height = 3 * EXT
        stack = jnp.concatenate(parts, axis=0)
        z_faces[0] = jnp.where(me_z > 0, z_low_in[...].astype(F32), 0.0)
        z_faces[1] = jnp.where(me_z < last_z, z_high_in[...].astype(F32), 0.0)
        y_first, y_second = first_in[...].astype(F32), second_in[...].astype(F32)
        y_faces[0] = jnp.where(even, y_first, y_second)
        y_faces[1] = jnp.where(even, y_second, y_first)
        source = iota((128, 128), 0)
        fine_z = iota((128, 128), 1).astype(F32)
        coarse_z = (source % 32 - 2).astype(F32)
        coarse_y = (source // 32 - 1).astype(F32)
        along_z = jnp.maximum(
            1.0 - jnp.abs(fine_z * 0.125 + (0.0625 - 0.5) - coarse_z), 0.0
        )
        for y in range(16):
            at = (y + 0.5) / 8.0 - 0.5
            along_y = jnp.maximum(0.5 - 0.5 * jnp.abs(at - coarse_y), 0.0)
            product = jnp.dot(
                stack, (along_z * along_y).astype(BF16), preferred_element_type=F32
            )
            field[pl.ds(y * height, height), :] = (
                product[:height] + product[height : 2 * height] + product[2 * height :]
            )

    height = 3 * EXT
    cells = chunk // 8
    lane = iota((16, 128), 1)
    row = iota((16, 128), 0)
    diag = (iota((128, 128), 0) == iota((128, 128), 1))
    z_from = iota((128, 128), 0)
    z_to = iota((128, 128), 1)
    difference = (
        jnp.where(z_from == z_to + 1, 1.0, 0.0) - jnp.where(z_from + 1 == z_to, 1.0, 0.0)
    ).astype(BF16)
    from_low = jnp.where(z_to == 0, -1.0, 0.0).astype(BF16)
    from_high = jnp.where(z_to == 127, 1.0, 0.0).astype(BF16)
    x_low = slab_in[lower, 24:40, :]
    x_low = jnp.where(me > 0, x_low, 0.0)
    x_high = slab_in[upper, 24:40, :]
    x_high = jnp.where(me < devices - 1, x_high, 0.0)
    before = jnp.where(step > 0, before_ref[0].astype(F32), x_low)
    after = jnp.where(step < pl.num_programs(0) - 1, after_ref[0].astype(F32), x_high)
    for c in range(cells):
        here = step * cells + c
        block = ref_ref[pl.ds(c * 8, 8)]
        flat = block.reshape(128, 128)
        low_line = z_faces[0, pl.ds(here, 1), :]
        high_line = z_faces[1, pl.ds(here, 1), :]
        low_diag = jnp.where(diag, low_line, 0.0).astype(BF16)
        high_diag = jnp.where(diag, high_line, 0.0).astype(BF16)
        grad_z = (
            jnp.dot(flat, difference, preferred_element_type=F32)
            + jnp.dot(low_diag, from_low, preferred_element_type=F32)
            + jnp.dot(high_diag, from_high, preferred_element_type=F32)
        )
        y_low = y_faces[0, pl.ds(pl.multiple_of(here * 8, 8), 8), :]
        y_high = y_faces[1, pl.ds(pl.multiple_of(here * 8, 8), 8), :]
        index_low = jnp.where(here > 0, here - 1, rows)
        index_high = jnp.where(here < rows - 1, here + 1, rows + 1)
        middle, to_low, to_high = [], [], []
        for k in range(3):
            own = field[pl.ds(k * EXT + here, 16, stride=height), :]
            middle.append(own)
            to_low.append(field[pl.ds(k * EXT + index_low, 16, stride=height), :] - own)
            to_high.append(field[pl.ds(k * EXT + index_high, 16, stride=height), :] - own)
        wide = [before if c == 0 else ref_ref[c * 8 - 1].astype(F32)]
        wide += [block[s].astype(F32) for s in range(8)]
        wide += [after if c == cells - 1 else ref_ref[c * 8 + 8].astype(F32)]
        for s in range(8):
            t = (s + 0.5) / 8.0 - 0.5
            side = to_low if t < 0 else to_high
            value = [middle[k] + abs(t) * side[k] for k in range(3)]
            own = wide[s + 1]
            y_up = jnp.where(row == 15, y_high[s : s + 1], roll(own, -1, 0))
            y_down = jnp.where(row == 0, y_low[s : s + 1], roll(own, 1, 0))
            total = def_ref[c * 8 + s].astype(F32) - own
            total = total - (wide[s + 2] - wide[s]) * value[0]
            total = total - (y_up - y_down) * value[1]
            total = total - grad_z[s * 16 : s * 16 + 16] * value[2]
            out_ref[c * 8 + s] = total.astype(BF16)


def solution(mesh):
    gx, gy, gz = (mesh.shape[a] for a in ("gx", "gy", "gz"))

    def pairs(even_up):
        out = []
        for y in range(gy):
            for z in range(gz):
                to = y + (1 if (z % 2 == 0) == even_up else -1)
                if 0 <= to < gy:
                    out.append((y * gz + z, to * gz + z))
        return out

    def on_device(ref_image, def_image, displacement):
        sizex, sizey, sizez = ref_image.shape
        rows = sizex // 8
        weights, table = solve_tables(gx, rows)
        chunk = 64
        steps = sizex // chunk
        disp = jnp.transpose(displacement, (0, 2, 3, 1))
        image_block = pl.BlockSpec((chunk, sizey, sizez), lambda i: (i, 0, 0))

        def whole(shape):
            return pl.BlockSpec(shape, lambda i: (0,) * len(shape))

        coarse_shape = (2, rows, 128)
        z_rows = 3 * rows + 32
        y_rows = 3 * rows + sizex
        coarse, up, down, y_high, y_low = pl.pallas_call(
            lambda *refs: bin_kernel(chunk, *refs),
            name="bin_and_pack",
            grid=(steps,),
            in_specs=[image_block, image_block, whole(disp.shape)],
            out_specs=[
                whole(coarse_shape), whole((z_rows, 128)), whole((z_rows, 128)),
                whole((sizex, 128)), whole((sizex, 128)),
            ],
            out_shape=[
                jax.ShapeDtypeStruct(coarse_shape, F32),
                jax.ShapeDtypeStruct((z_rows, 128), BF16),
                jax.ShapeDtypeStruct((z_rows, 128), BF16),
                jax.ShapeDtypeStruct((sizex, 128), BF16),
                jax.ShapeDtypeStruct((sizex, 128), BF16),
            ],
            scratch_shapes=[pltpu.VMEM((2, 2, rows, 128), F32), pltpu.VMEM((2, 32, 128), F32)],
        )(ref_image, def_image, disp)
        z_low = lax.ppermute(up, "gz", [(i, (i + 1) % gz) for i in range(gz)])
        z_high = lax.ppermute(down, "gz", [((i + 1) % gz, i) for i in range(gz)])
        coarse, first, second = pl.pallas_call(
            lambda *refs: z_kernel(gz, *refs),
            name="extend_along_z",
            in_specs=[VMEM] * 5,
            out_specs=[VMEM] * 3,
            out_shape=[
                jax.ShapeDtypeStruct(coarse_shape, F32),
                jax.ShapeDtypeStruct((y_rows, 128), BF16),
                jax.ShapeDtypeStruct((y_rows, 128), BF16),
            ],
        )(coarse, z_low, z_high, y_high, y_low)
        first = lax.ppermute(first, ("gy", "gz"), pairs(True))
        second = lax.ppermute(second, ("gy", "gz"), pairs(False))
        plane = (1, sizey, sizez)
        slabs, rhs, disp = pl.pallas_call(
            rhs_kernel,
            name="right_hand_sides",
            grid=(1,),
            in_specs=[
                whole(coarse_shape), whole((y_rows, 128)), whole((y_rows, 128)),
                pl.BlockSpec(plane, lambda i: (0, 0, 0)),
                pl.BlockSpec(plane, lambda i: (sizex - 1, 0, 0)),
                whole(weights.shape),
            ],
            out_specs=[
                whole((gx, SLAB, 128)), whole((3, rows, 128)), whole((3, rows, 128)),
            ],
            out_shape=[
                jax.ShapeDtypeStruct((gx, SLAB, 128), F32),
                jax.ShapeDtypeStruct((3, rows, 128), F32),
                jax.ShapeDtypeStruct((3, rows, 128), F32),
            ],
        )(coarse, first, second, ref_image, ref_image, jnp.asarray(weights))
        slabs = lax.all_to_all(slabs, "gx", 0, 0, tiled=True)
        z_block = pl.BlockSpec((32, 128), lambda i: (3, 0))
        new, residual = pl.pallas_call(
            lambda *refs: fine_kernel(
                chunk, *refs[:6],
                refs[6].at[pl.ds(3 * rows, sizex)], refs[7].at[pl.ds(3 * rows, sizex)],
                *refs[8:],
            ),
            name="solve_and_residual",
            grid=(steps,),
            in_specs=[
                whole((gx, SLAB, 128)), whole((3, rows, 128)), whole((3, rows, 128)),
                whole(table.shape), z_block, z_block,
                whole((y_rows, 128)), whole((y_rows, 128)),
                image_block,
                pl.BlockSpec(plane, lambda i: (jnp.maximum(i * chunk - 1, 0), 0, 0)),
                pl.BlockSpec(plane, lambda i: (jnp.minimum(i * chunk + chunk, sizex - 1), 0, 0)),
                image_block,
            ],
            out_specs=[whole((3, 2, 16, rows)), image_block],
            out_shape=[
                jax.ShapeDtypeStruct((3, 2, 16, rows), F32),
                jax.ShapeDtypeStruct(ref_image.shape, BF16),
            ],
            scratch_shapes=[
                pltpu.VMEM((16 * 3 * EXT, 128), F32),
                pltpu.VMEM((2, rows, 128), F32),
                pltpu.VMEM((2, sizex, 128), F32),
            ],
        )(
            slabs, rhs, disp, jnp.asarray(table), z_low, z_high, first, second,
            ref_image, ref_image, ref_image, def_image,
        )
        return jnp.transpose(new, (0, 3, 1, 2)), residual

    return jax.shard_map(
        on_device,
        mesh=mesh,
        in_specs=(P("gx", "gy", "gz"), P("gx", "gy", "gz"), P(None, "gx", "gy", "gz")),
        out_specs=(P(None, "gx", "gy", "gz"), P("gx", "gy", "gz")),
        check_vma=False,
    )
```

time: 306 us -> 59.3 us (0.19)
  the two profiles are of different devices: /device:TPU:18 before, /device:TPU:6 now
where the time goes in v1:
time: 59.3 us; the launch traced here: 58.6 us
  waiting for transfers between devices  18.5 us (31%)
  Pallas kernels  14.7 us (25%)
  blocking collectives  14.7 us (25%)
  starting transfers between devices  8.9 us (15%)
  local copies, waits for them, and re-layouts  1.23 us (2%)
  between operations  0.65 us (1%)
    all_to_all x1, blocking collectives, on_device(): slabs = lax.all_to_all(slabs, 'gx', 0, 0, tiled=True)  14.7 us
    ppermute x1, waiting for transfers between devices, on_device(): second = lax.ppermute(second, ('gy', 'gz'), pairs(False))  12.3 us
    pallas_call x1, Pallas kernels, on_device(): pl.pallas_call(lambda *refs: fine_kernel(chunk, *refs[:6], refs[6].at[pl....  6.84 us
    ppermute x1, starting transfers between devices, on_device(): first = lax.ppermute(first, ('gy', 'gz'), pairs(True))  5.87 us
    pallas_call x1, Pallas kernels, on_device(): pl.pallas_call(lambda *refs: bin_kernel(chunk, *refs), name='bin_and_pack...  4 us
    ppermute x1, waiting for transfers between devices, on_device(): z_high = lax.ppermute(down, 'gz', [((i + 1) % gz, i) for i in range(gz)])  3.33 us
    pallas_call x1, Pallas kernels, on_device(): pl.pallas_call(rhs_kernel, name='right_hand_sides', grid=(1,), in_specs=[...  2.08 us
    ppermute x1, waiting for transfers between devices, on_device(): z_low = lax.ppermute(up, 'gz', [(i, (i + 1) % gz) for i in range(gz)])  1.8 us
  transfers between devices with their start and end apart: 4, of which 4 were waited for; matrix products, arithmetic and copies ran while one was open for 0% of the time, Pallas kernels for 0%

profile of v1, /device:TPU:6, one launch (start us, length us, event | category | flops | bytes accessed | tf_op | source)
XLA Modules:
  0.0 58.6 jit_solution(7245392884877588333)
XLA Ops:
  0.6 4.0 %bin_and_pack.1 = (f32[2,32,128]{2,1,0:T(8,128)}, bf16[128,128]{1,0:T(8,128)(2,1)}, bf16[128,128]{1,0:T(8,128)(2,1)}, bf16[256,128]{1,0:T(8,128)(2,1)}, bf16[256,128]{1,0:T(8,128)(2,1)}) custom-call(bf16[256,16,128]{2,1,0:T(8,128)(2,1)} %refs_10_.1, bf16[256,16,128]{2,1,0:T(8,128)(2,1)} %refs_11_.1, f32[3,2,16,32]{3,2,1,0:T(8,128)} %bitcast.2), custom_call_target="tpu_custom_call" | custom-call | tf_op jit(solution)/shard_map/bin_and_pack/pallas_call | solution.py:415
  4.6 0.0 collective-permute-start
  4.6 1.7 %collective-permute-start.1 = (bf16[128,128]{1,0:T(8,128)(2,1)}, bf16[128,128]{1,0:T(8,128)(2,1)S(1)}, u32[]{:S(2)}, u32[]{:S(2)}) collective-permute-start(bf16[128,128]{1,0:T(8,128)(2,1)} %get-tuple-element.17), channel_id=1, source_target_pairs={{1,0},{2,1},{3,2},{4,3},{5,4},{6,5},{7,6},{0,7},{9,8},{10,9},{11,1... | collective-permute-start | bytes 98312 | tf_op jit(solution)/shard_map/ppermute | solution.py:434
  6.4 1.8 %collective-permute-done.refs_1_.refs_4_ = bf16[128,128]{1,0:T(8,128)(2,1)S(1)} collective-permute-done((bf16[128,128]{1,0:T(8,128)(2,1)}, bf16[128,128]{1,0:T(8,128)(2,1)S(1)}, u32[]{:S(2)}, u32[]{:S(2)}) %collective-permute-start) | collective-permute-done | bytes 32800 | tf_op jit(solution)/shard_map/ppermute | solution.py:433
  8.2 0.0 copy-start.2
  8.2 3.3 %collective-permute-done.1.refs_2_.refs_5_ = bf16[128,128]{1,0:T(8,128)(2,1)S(1)} collective-permute-done((bf16[128,128]{1,0:T(8,128)(2,1)}, bf16[128,128]{1,0:T(8,128)(2,1)S(1)}, u32[]{:S(2)}, u32[]{:S(2)}) %collective-permute-start.1) | collective-permute-done | bytes 32800 | tf_op jit(solution)/shard_map/ppermute | solution.py:434
  11.5 0.0 copy-start.3
  11.5 0.0 copy-done.2
  11.5 0.6 %copy-done.3 = bf16[128,128]{1,0:T(8,128)(2,1)} copy-done((bf16[128,128]{1,0:T(8,128)(2,1)}, bf16[128,128]{1,0:T(8,128)(2,1)S(1)}, u32[]{:S(2)}) %copy-start.3) | copy-done | bytes 32792
  12.1 1.8 %extend_along_z.1 = (f32[2,32,128]{2,1,0:T(8,128)}, bf16[352,128]{1,0:T(8,128)(2,1)}, bf16[352,128]{1,0:T(8,128)(2,1)}) custom-call(f32[2,32,128]{2,1,0:T(8,128)} %get-tuple-element.15.refs_0_, bf16[128,128]{1,0:T(8,128)(2,1)} %copy-done.2, bf16[128,128]{1,0:T(8,128)(2,1)} %copy-done.3, bf16[256,128]{1,0:T(8,128)(2,1)} %get-tuple-element.18.refs_3_, ...), custom_call_target="tpu_custom_call" | custom-call | tf_op jit(solution)/shard_map/extend_along_z/pallas_call | solution.py:435
  13.9 5.9 %collective-permute-start.2 = (bf16[352,128]{1,0:T(8,128)(2,1)}, bf16[352,128]{1,0:T(8,128)(2,1)S(1)}, u32[]{:S(2)}, u32[]{:S(2)}) collective-permute-start(bf16[352,128]{1,0:T(8,128)(2,1)} %get-tuple-element.21), channel_id=1, source_target_pairs={{0,8},{2,10},{4,12},{6,14},{8,16},{9,1},{10,18},{11,3},{12,20},{13... | collective-permute-start | bytes 270344 | tf_op jit(solution)/shard_map/ppermute | solution.py:446
  19.7 1.3 %collective-permute-start.3 = (bf16[352,128]{1,0:T(8,128)(2,1)}, bf16[352,128]{1,0:T(8,128)(2,1)S(1)}, u32[]{:S(2)}, u32[]{:S(2)}) collective-permute-start(bf16[352,128]{1,0:T(8,128)(2,1)} %get-tuple-element.22), channel_id=1, source_target_pairs={{1,9},{3,11},{5,13},{7,15},{8,0},{9,17},{10,2},{11,19},{12,4},{13,... | collective-permute-start | bytes 270344 | tf_op jit(solution)/shard_map/ppermute | solution.py:447
  21.0 1.1 %collective-permute-done.2.first_in.refs_6_ = bf16[352,128]{1,0:T(8,128)(2,1)S(1)} collective-permute-done((bf16[352,128]{1,0:T(8,128)(2,1)}, bf16[352,128]{1,0:T(8,128)(2,1)S(1)}, u32[]{:S(2)}, u32[]{:S(2)}) %collective-permute-start.2) | collective-permute-done | bytes 90144 | tf_op jit(solution)/shard_map/ppermute | solution.py:446
  22.2 0.0 copy-start
  22.2 12.3 %collective-permute-done.3.second_in.refs_7_ = bf16[352,128]{1,0:T(8,128)(2,1)S(1)} collective-permute-done((bf16[352,128]{1,0:T(8,128)(2,1)}, bf16[352,128]{1,0:T(8,128)(2,1)S(1)}, u32[]{:S(2)}, u32[]{:S(2)}) %collective-permute-start.3) | collective-permute-done | bytes 90144 | tf_op jit(solution)/shard_map/ppermute | solution.py:447
  34.4 0.0 copy-start.1
  34.4 0.0 copy-done
  34.5 0.6 %copy-done.1 = bf16[352,128]{1,0:T(8,128)(2,1)} copy-done((bf16[352,128]{1,0:T(8,128)(2,1)}, bf16[352,128]{1,0:T(8,128)(2,1)S(1)}, u32[]{:S(2)}) %copy-start.1) | copy-done | bytes 90136
  35.1 2.1 %right_hand_sides.1 = (f32[16,40,128]{2,1,0:T(8,128)}, f32[3,32,128]{2,1,0:T(8,128)}, f32[3,32,128]{2,1,0:T(8,128)}) custom-call(f32[2,32,128]{2,1,0:T(8,128)} %get-tuple-element.20.coarse_in, bf16[352,128]{1,0:T(8,128)(2,1)} %copy-done, bf16[352,128]{1,0:T(8,128)(2,1)} %copy-done.1, bf16[256,16,128]{2,1,0:T(8,128)(2,1)} %refs_10_.1, ...), custom_call_target="tpu_custom_call" | custom-call | tf_op jit(solution)/shard_map/right_hand_sides/pallas_call | solution.py:449
  37.2 14.7 %all_to_all.5.refs_0_ = f32[16,40,128]{2,1,0:T(8,128)} all-to-all(f32[16,40,128]{2,1,0:T(8,128)} %get-tuple-element.23), channel_id=1, replica_groups=mesh['gx'=16,'gy'=4,'gz'=8] {'gx'}, dimensions={0} | all-to-all | bytes 655360 | tf_op jit(solution)/shard_map/all_to_all | solution.py:468
  51.8 6.8 %solve_and_residual.1 = (f32[3,2,16,32]{3,2,1,0:T(8,128)}, bf16[256,16,128]{2,1,0:T(8,128)(2,1)}) custom-call(f32[16,40,128]{2,1,0:T(8,128)} %all_to_all.5.refs_0_, f32[3,32,128]{2,1,0:T(8,128)} %get-tuple-element.24.refs_1_, f32[3,32,128]{2,1,0:T(8,128)} %get-tuple-element.25.refs_2_, f32[16,40,96]{2,1,0:T(8,128)} %constant.5.clone.refs_3_, ...), custom_call_target="tpu_custom_call" | custom-call | tf_op jit(solution)/shard_map/solve_and_residual/pallas_call | solution.py:470
Async XLA Ops:
  4.6 3.6 %collective-permute-start = (bf16[128,128]{1,0:T(8,128)(2,1)}, bf16[128,128]{1,0:T(8,128)(2,1)S(1)}, u32[]{:S(2)}, u32[]{:S(2)}) collective-permute-start(bf16[128,128]{1,0:T(8,128)(2,1)} %get-tuple-element.16), channel_id=1, source_target_pairs={{0,1},{1,2},{2,3},{3,4},{4,5},{5,6},{6,7},{7,0},{8,9},{9,10},{10,1... | collective-permute-start | bytes 98312 | tf_op jit(solution)/shard_map/ppermute | solution.py:433
  4.6 6.9 %collective-permute-start.1 = (bf16[128,128]{1,0:T(8,128)(2,1)}, bf16[128,128]{1,0:T(8,128)(2,1)S(1)}, u32[]{:S(2)}, u32[]{:S(2)}) collective-permute-start(bf16[128,128]{1,0:T(8,128)(2,1)} %get-tuple-element.17), channel_id=1, source_target_pairs={{1,0},{2,1},{3,2},{4,3},{5,4},{6,5},{7,6},{0,7},{9,8},{10,9},{11,1... | collective-permute-start | bytes 98312 | tf_op jit(solution)/shard_map/ppermute | solution.py:434
  8.2 3.3 %copy-start.2 = (bf16[128,128]{1,0:T(8,128)(2,1)}, bf16[128,128]{1,0:T(8,128)(2,1)S(1)}, u32[]{:S(2)}) copy-start(bf16[128,128]{1,0:T(8,128)(2,1)S(1)} %collective-permute-done.refs_1_.refs_4_) | copy-start | bytes 98308
  11.5 0.6 %copy-start.3 = (bf16[128,128]{1,0:T(8,128)(2,1)}, bf16[128,128]{1,0:T(8,128)(2,1)S(1)}, u32[]{:S(2)}) copy-start(bf16[128,128]{1,0:T(8,128)(2,1)S(1)} %collective-permute-done.1.refs_2_.refs_5_) | copy-start | bytes 98308
  13.9 8.3 %collective-permute-start.2 = (bf16[352,128]{1,0:T(8,128)(2,1)}, bf16[352,128]{1,0:T(8,128)(2,1)S(1)}, u32[]{:S(2)}, u32[]{:S(2)}) collective-permute-start(bf16[352,128]{1,0:T(8,128)(2,1)} %get-tuple-element.21), channel_id=1, source_target_pairs={{0,8},{2,10},{4,12},{6,14},{8,16},{9,1},{10,18},{11,3},{12,20},{13... | collective-permute-start | bytes 270344 | tf_op jit(solution)/shard_map/ppermute | solution.py:446
  19.7 14.7 %collective-permute-start.3 = (bf16[352,128]{1,0:T(8,128)(2,1)}, bf16[352,128]{1,0:T(8,128)(2,1)S(1)}, u32[]{:S(2)}, u32[]{:S(2)}) collective-permute-start(bf16[352,128]{1,0:T(8,128)(2,1)} %get-tuple-element.22), channel_id=1, source_target_pairs={{1,9},{3,11},{5,13},{7,15},{8,0},{9,17},{10,2},{11,19},{12,4},{13,... | collective-permute-start | bytes 270344 | tf_op jit(solution)/shard_map/ppermute | solution.py:447
  22.2 12.3 %copy-start = (bf16[352,128]{1,0:T(8,128)(2,1)}, bf16[352,128]{1,0:T(8,128)(2,1)S(1)}, u32[]{:S(2)}) copy-start(bf16[352,128]{1,0:T(8,128)(2,1)S(1)} %collective-permute-done.2.first_in.refs_6_) | copy-start | bytes 270340
  34.4 0.6 %copy-start.1 = (bf16[352,128]{1,0:T(8,128)(2,1)}, bf16[352,128]{1,0:T(8,128)(2,1)S(1)}, u32[]{:S(2)}) copy-start(bf16[352,128]{1,0:T(8,128)(2,1)S(1)} %collective-permute-done.3.second_in.refs_7_) | copy-start | bytes 270340

commit v2 on v1

v2 whole, which is shorter than its diff:
```python
import numpy as np
import jax
import jax.numpy as jnp
from jax import lax
from jax.experimental import pallas as pl
from jax.experimental.pallas import tpu as pltpu
from jax.sharding import PartitionSpec as P

STIFFNESS = 64.0
SPAN = 20
VMEM = pl.BlockSpec(memory_space=pltpu.VMEM)
HBM = pl.BlockSpec(memory_space=pltpu.HBM)
HIGHEST = lax.Precision.HIGHEST
F32 = jnp.float32
BF16 = jnp.bfloat16
SLAB = 48
VMEM_BYTES = 16 * 2**20
EXT = 40


def inverse_entry(lines):
    diagonal = 1.0 + 2.0 * STIFFNESS
    root = (diagonal - np.sqrt(diagonal**2 - 4.0 * STIFFNESS**2)) / (2.0 * STIFFNESS)
    theta = -np.log(root)
    scale = 1.0 / (2.0 * STIFFNESS * np.sinh(theta) * (1.0 - root ** (2.0 * (lines + 1))))

    def first(i):
        return 1.0 - root ** (2.0 * (i + 1))

    def last(i):
        return 1.0 - root ** (2.0 * (lines - i))

    return root, scale, first, last


def solve_tables(devices, cells):
    lines = devices * cells
    root, scale, first, last = inverse_entry(lines)
    local = np.arange(cells)
    weights = np.zeros((devices, 8, cells))
    table = np.zeros((devices, EXT, cells + 3 * devices))
    everyone = np.arange(devices)
    for p in range(devices):
        at = p * cells + local
        weights[p, 0] = first(at) * root ** (cells - 1.0 - local)
        weights[p, 1] = last(at) * root**local
        rows = np.concatenate([at, [p * cells - 1, p * cells + cells]])[:, None]
        used = slice(0, cells + 2)

        def entry(columns):
            low, high = np.minimum(rows, columns), np.maximum(rows, columns)
            return scale * root ** (1.0 * (high - low)) * first(low) * last(high)

        table[p, used, :cells] = entry(at[None, :])
        below, above = (everyone < p)[None, :], (everyone > p)[None, :]
        gap = np.where(below, rows - (everyone * cells + cells - 1)[None, :], 0)
        sums = below * last(rows) * root ** (1.0 * gap)
        gap = np.where(above, (everyone * cells)[None, :] - rows, 0)
        sums += above * first(rows) * root ** (1.0 * gap)
        table[p, used, cells : cells + devices] = scale * sums
        table[p, used, cells + devices : cells + 2 * devices] = entry((everyone * cells)[None, :])
        table[p, used, cells + 2 * devices :] = entry((everyone * cells + cells - 1)[None, :])
    return weights.astype(np.float32), table.astype(np.float32)


def prolong_table(sizey, sizez):
    lane = np.arange(128)[:, None]
    coarse_y, coarse_z = lane // SPAN - 1, lane % SPAN - 2

    def tent(fine, coarse):
        return np.maximum(1.0 - np.abs((fine + 0.5) / 8.0 - 0.5 - coarse), 0.0)

    along_y = tent(np.arange(sizey)[None, :], coarse_y) * (lane < 4 * SPAN)
    along_z = tent(np.arange(sizez)[None, :], coarse_z)
    product = 0.5 * along_y[:, :, None] * along_z[:, None, :]
    return product.reshape(128, sizey * sizez).astype(BF16)


def iota(shape, dim):
    return lax.broadcasted_iota(jnp.int32, shape, dim)


def roll(value, shift, axis):
    size = value.shape[axis]
    return pltpu.roll(value, shift % size, axis)


def exact_dot(a, b, dims):
    return lax.dot_general(a, b, (dims, ((), ())), precision=HIGHEST, preferred_element_type=F32)


def put_split(ref, start, value):
    rows = value.shape[0]
    for part in range(3):
        piece = value.astype(BF16)
        ref[pl.ds(start + part * rows, rows), :] = piece
        value = value - piece.astype(F32)


def get_split(ref, rows):
    return (
        ref[0:rows, :].astype(F32)
        + ref[rows : 2 * rows, :].astype(F32)
        + ref[2 * rows : 3 * rows, :].astype(F32)
    )


def bin_kernel(
    chunk, ref_hbm, def_hbm, disp_hbm,
    coarse_ref, up_ref, down_ref, y_high_ref, y_low_ref,
    ref_buf, def_buf, disp_buf, bins, faces, sems, disp_sem,
):
    cells = chunk // 8
    steps = ref_buf.shape[0] // chunk

    def copy(k, step):
        source, target = ((ref_hbm, ref_buf), (def_hbm, def_buf))[k]
        planes = pl.ds(step * chunk, chunk)
        return pltpu.make_async_copy(source.at[planes], target.at[planes], sems.at[k, step])

    disp_copy = pltpu.make_async_copy(disp_hbm, disp_buf, disp_sem)
    for step in range(steps):
        copy(0, step).start()
        copy(1, step).start()
    disp_copy.start()
    lane = iota((16, 128), 1)
    row = iota((16, 128), 0)
    pick = jnp.where(
        ((row == 0) & (lane == 127)) | ((row == 1) & (lane == 0)), 1.0, 0.0
    ).astype(BF16)
    for step in range(steps):
        x0, row0 = step * chunk, step * cells
        for k, image in enumerate((ref_buf, def_buf)):
            copy(k, step).wait()
            for c in range(cells):
                total = image[pl.ds(x0 + c * 8, 8)].astype(F32).sum(0)
                for y in range(2):
                    bins[k, y, row0 + c : row0 + c + 1, :] = total[y * 8 : y * 8 + 8].sum(
                        0, keepdims=True
                    )
        flat = ref_buf[pl.ds(x0, chunk)].reshape(chunk * 16, 128)
        sides = lax.dot_general(
            pick, flat, (((1,), (1,)), ((), ())), preferred_element_type=F32
        )
        for c in range(cells):
            at = row0 + c
            faces[0, at : at + 1, :] = sides[0:1, c * 128 : (c + 1) * 128]
            faces[1, at : at + 1, :] = sides[1:2, c * 128 : (c + 1) * 128]
        wide = ref_buf[pl.ds(x0, chunk)].astype(F32)
        y_high_ref[pl.ds(x0, chunk), :] = wide[:, 15, :].astype(BF16)
        y_low_ref[pl.ds(x0, chunk), :] = wide[:, 0, :].astype(BF16)
    disp_copy.wait()
    rows = bins.shape[2]
    z = iota((128, 128), 0) // 8
    lanes = iota((128, 128), 1)
    place_lanes = iota((16, 128), 1)
    place_z = iota((16, 128), 0)
    whole = []
    for y in range(2):
        total = jnp.zeros((rows, 128), F32)
        for k in range(2):
            summer = jnp.where(lanes == k * SPAN + 2 + z, 1.0 / 32.0, 0.0)
            total += exact_dot(bins[k, y], summer, ((1,), (0,)))
        for k in range(3):
            place = jnp.where(place_lanes == (2 + k) * SPAN + 2 + place_z, 1.0, 0.0)
            total += exact_dot(disp_buf[k, y], place, ((0,), (0,)))
        coarse_ref[y] = total
        whole.append(total)
    position = iota((rows, 128), 1) % SPAN
    up = jnp.where(position < 2, roll(whole[0], -16, 1), roll(whole[1], -12, 1))
    down = jnp.where(position >= 18, roll(whole[0], 16, 1), roll(whole[1], 12, 1))
    put_split(up_ref, 0, up)
    put_split(down_ref, 0, down)
    up_ref[pl.ds(3 * rows, 32), :] = faces[0].astype(BF16)
    down_ref[pl.ds(3 * rows, 32), :] = faces[1].astype(BF16)


def z_kernel(
    devices, coarse_in, low_in, high_in, y_high_in, y_low_in, coarse_out, down_out, up_out
):
    rows = coarse_in.shape[1]
    me = lax.axis_index("gz")
    lane = iota((rows, 128), 1)
    position = lane % SPAN
    inside = lane < 5 * SPAN
    low = jnp.where(me > 0, get_split(low_in, rows), 0.0)
    high = jnp.where(me < devices - 1, get_split(high_in, rows), 0.0)
    whole = []
    for y in range(2):
        value = coarse_in[y]
        value = jnp.where((position < 2) & inside, roll(low, -4 * y, 1), value)
        value = jnp.where((position >= 18) & inside, roll(high, 4 * y, 1), value)
        coarse_out[y] = value
        whole.append(value)
    up = jnp.where(inside, whole[1], roll(whole[0], 100, 1))
    down = jnp.where(inside, whole[0], roll(whole[1], 100, 1))
    put_split(down_out, 0, down)
    put_split(up_out, 0, up)
    fine = y_high_in.shape[0]
    down_out[pl.ds(3 * rows, fine), :] = y_low_in[...]
    up_out[pl.ds(3 * rows, fine), :] = y_high_in[...]


def rhs_kernel(
    coarse_in, above_in, below_in, ref_in, weights_in,
    slab_out, rhs_out, disp_out,
):
    rows = coarse_in.shape[1]
    devices = slab_out.shape[0]
    me = lax.axis_index("gx")
    below, above = get_split(below_in, rows), get_split(above_in, rows)
    layers = [below, coarse_in[0], coarse_in[1], above]
    lane = iota((rows, 128), 1)
    group = lane // SPAN
    position = lane % SPAN
    row = iota((rows, 128), 0)

    def packed(sources):
        value = jnp.zeros((rows, 128), F32)
        for y, (layer, at) in enumerate(sources):
            value = jnp.where(group == y, roll(layer, SPAN * y - at, 1), value)
        return value

    cell = packed([(layer, 0) for layer in layers])
    cell_below = packed([(below, 100), (layers[0], 0), (layers[1], 0), (layers[2], 0)])
    cell_above = packed([(layers[1], 0), (layers[2], 0), (layers[3], 0), (above, 100)])
    cell_def = packed([(layer, SPAN) for layer in layers])
    disp = [packed([(layer, (2 + k) * SPAN) for layer in layers]) for k in range(3)]
    slope_y = (cell_above - cell_below) * 0.5
    slope_z = (roll(cell, -1, 1) - roll(cell, 1, 1)) * 0.5
    slope_x = (roll(cell, -1, 0) - roll(cell, 1, 0)) * 0.5
    partial = cell_def - cell - (slope_y * disp[1] + slope_z * disp[2])
    mismatch = partial - slope_x * disp[0]
    keep = (position >= 1) & (position < SPAN - 1) & (row > 0) & (row < rows - 1)
    keep &= lane < 4 * SPAN
    weights = weights_in[me]
    sums = []
    for k, slope in enumerate((slope_x, slope_y, slope_z)):
        rhs = jnp.where(keep, slope * mismatch, 0.0)
        rhs_out[k] = rhs
        disp_out[k] = disp[k]
        sums.append(exact_dot(weights, rhs, ((1,), (0,))))
    end = rows - 1
    shared = [cell[i : i + 1] for i in (0, 1, end - 1, end)]
    shared += [partial[0:1], partial[end:], disp[0][0:1], disp[0][end:], slope_y[0:1]]
    shared_more = [slope_y[end:], slope_z[0:1], slope_z[end:]]
    zero = jnp.zeros((1, 128), F32)
    lane = iota((12, 128), 1)

    def message(sum_row, edge):
        main = jnp.concatenate([s[sum_row : sum_row + 1] for s in sums] + shared, axis=0)
        edges = [disp[1][edge : edge + 1], disp[2][edge : edge + 1], zero]
        more = jnp.concatenate(shared_more + edges, axis=0)
        more = jnp.concatenate([roll(more, 4 * SPAN, 1), roll(more, 2 * SPAN, 1)], axis=0)
        rest = jnp.where(lane < 4 * SPAN, main, more)
        pieces = []
        for _ in range(3):
            piece = rest.astype(BF16).astype(F32)
            pieces.append(piece)
            rest = rest - piece
        return jnp.concatenate([pieces[0], pieces[1], pieces[2][:8]], axis=0).astype(BF16)

    to_above, to_below = message(0, end), message(1, 0)
    low_plane, high_plane = ref_in[0], ref_in[ref_in.shape[0] - 1]
    for q in range(devices):
        slab_out[q, 0:16, :] = jnp.where(me > q, low_plane, high_plane)
        slab_out[q, 16:48, :] = jnp.where(me > q, to_below, to_above)


def fine_kernel(
    slab_in, rhs_in, disp_in, table_in, prolong_in, z_low_in, z_high_in, above_in, below_in,
    ref_in, def_in,
    disp_out, out_hbm,
    lines, field, z_faces, out_buf, sems,
):
    devices = slab_in.shape[0]
    rows = rhs_in.shape[1]
    me = lax.axis_index("gx")
    me_z = lax.axis_index("gz")
    last_z = lax.axis_size("gz") - 1
    height = 3 * EXT
    lines[...] = slab_in[:, 16:48, :].astype(F32)
    lane = iota((devices, 128), 1)
    q = iota((devices, 128), 0)
    keep = (lane % SPAN >= 1) & (lane % SPAN < SPAN - 1) & (lane < 4 * SPAN)

    def whole_line(i):
        value = lines[:, i, :] + lines[:, 12 + i, :]
        return value + lines[:, 24 + i, :] if i < 8 else value

    full = [whole_line(i) for i in range(12)]
    more = [
        jnp.where(lane < 2 * SPAN, roll(full[i], -4 * SPAN, 1), roll(full[6 + i], -2 * SPAN, 1))
        for i in range(5)
    ]
    cell_0, cell_1, cell_30, cell_31 = full[3:7]
    from_below = jnp.where(q > 0, roll(cell_31, 1, 0), 0.0)
    from_above = jnp.where(q < devices - 1, roll(cell_0, -1, 0), 0.0)
    slopes_0 = ((cell_1 - from_below) * 0.5, full[11], more[1])
    slopes_1 = ((from_above - cell_30) * 0.5, more[0], more[2])
    mismatch_0 = full[7] - slopes_0[0] * full[9]
    mismatch_1 = full[8] - slopes_1[0] * full[10]
    known = []
    for k in range(3):
        edge_0 = jnp.where(keep, slopes_0[k] * mismatch_0, 0.0)
        edge_1 = jnp.where(keep, slopes_1[k] * mismatch_1, 0.0)
        known.append(jnp.concatenate([rhs_in[k], full[k], edge_0, edge_1], axis=0))
    moved = exact_dot(table_in[me], jnp.concatenate(known, axis=1), ((1,), (0,)))

    def one(value, at):
        return jnp.where(q == at, value, 0.0).sum(0, keepdims=True)

    edge = iota((EXT - rows, 128), 0)
    block_lane = iota((EXT, 128), 1)
    block_keep = (block_lane % SPAN >= 1) & (block_lane % SPAN < SPAN - 1)
    block_keep &= block_lane < 4 * SPAN
    solved, inner = [], []
    for k in range(3):
        low_row = one((full[10], more[3], more[4])[k], me - 1)
        high_row = one((full[9], more[3], more[4])[k], me + 1)
        outer = jnp.where(edge == 0, low_row, jnp.where(edge == 1, high_row, 0.0))
        before = jnp.concatenate([disp_in[k], outer], axis=0)
        after = jnp.where(block_keep, before + moved[:, k * 128 : k * 128 + 128], 0.0)
        solved.append(after)
        inner.append(after[:rows])
    whole = jnp.concatenate(solved, axis=0)
    high = whole.astype(BF16)
    low = (whole - high.astype(F32)).astype(BF16)
    for y in range(0, 16, 2):
        table = prolong_in[:, y * 128 : y * 128 + 256]
        product = jnp.dot(high, table, preferred_element_type=F32) + jnp.dot(
            low, table, preferred_element_type=F32
        )
        field[y * height : (y + 1) * height, :] = product[:, :128]
        field[(y + 1) * height : (y + 2) * height, :] = product[:, 128:]
    own_lane, own_row = iota((32, 128), 1), iota((32, 128), 0)
    pick = jnp.where(own_lane == SPAN * (own_row // 16 + 1) + 2 + own_row % 16, 1.0, 0.0)
    placed = exact_dot(pick, jnp.concatenate(inner, axis=0), ((1,), (1,)))
    for k in range(3):
        for y in range(2):
            disp_out[k, y] = placed[16 * y : 16 * y + 16, k * rows : (k + 1) * rows]

    z_faces[0] = jnp.where(me_z > 0, z_low_in[3 * rows :, :].astype(F32), 0.0)
    z_faces[1] = jnp.where(me_z < last_z, z_high_in[3 * rows :, :].astype(F32), 0.0)
    eye = jnp.where(iota((128, 128), 0) == iota((128, 128), 1), 1.0, 0.0).astype(BF16)
    z_from, z_to = iota((384, 128), 0), iota((384, 128), 1)
    z_table = jnp.where((z_from == z_to + 1) & (z_from < 128), 1.0, 0.0)
    z_table -= jnp.where(z_from + 1 == z_to, 1.0, 0.0)
    z_table -= jnp.where((z_from >= 128) & (z_from < 256) & (z_to == 0), 1.0, 0.0)
    z_table += jnp.where((z_from >= 256) & (z_to == 127), 1.0, 0.0)
    z_table = z_table.astype(BF16)
    y_to, y_from = iota((128, 160), 0), iota((128, 160), 1)
    y_tables = []
    for half in range(2):
        low_at = 128 + 8 * half + y_to // 16
        plus = jnp.where(y_to % 16 == 15, low_at + 16, y_to + 1)
        minus = jnp.where(y_to % 16 == 0, low_at, y_to - 1)
        y_table = jnp.where(y_from == plus, 1.0, 0.0) - jnp.where(y_from == minus, 1.0, 0.0)
        y_tables.append(y_table.astype(BF16))
    x_low = slab_in[jnp.maximum(me - 1, 0), 0:16, :].astype(F32)
    x_low = jnp.where(me > 0, x_low, 0.0)
    x_high = slab_in[jnp.minimum(me + 1, devices - 1), 0:16, :].astype(F32)
    x_high = jnp.where(me < devices - 1, x_high, 0.0)
    cells = 4
    sizex = ref_in.shape[0]
    steps = rows // cells

    def send(step):
        planes = pl.ds(step * cells * 8, cells * 8)
        return pltpu.make_async_copy(out_buf.at[planes], out_hbm.at[planes], sems.at[step])

    def body(step, _):
        x0 = step * (cells * 8)
        before = ref_in[jnp.maximum(x0 - 1, 0)].astype(F32)
        before = jnp.where(step > 0, before, x_low)
        after = ref_in[jnp.minimum(x0 + cells * 8, sizex - 1)].astype(F32)
        after = jnp.where(step < steps - 1, after, x_high)
        y_rows = pl.ds(pl.multiple_of(3 * rows + x0, 32), cells * 8)
        y_lows = below_in[y_rows, :]
        y_highs = above_in[y_rows, :]
        index_low = jnp.where(step > 0, step * cells - 1, rows)
        index_high = jnp.where(step < steps - 1, step * cells + cells, rows + 1)
        indices = [index_low] + [step * cells + c for c in range(cells)] + [index_high]
        nodes = [
            [field[pl.ds(k * EXT + i, 16, stride=height), :] for k in range(3)] for i in indices
        ]
        slope = [(nodes[1][k] - nodes[0][k]) * 0.125 for k in range(3)]
        for c in range(cells):
            here = step * cells + c
            block = ref_in[pl.ds(x0 + c * 8, 8)]
            flat = block.reshape(128, 128)
            low_line = jnp.broadcast_to(z_faces[0, pl.ds(here, 1), :], (16, 128)).astype(BF16)
            high_line = jnp.broadcast_to(z_faces[1, pl.ds(here, 1), :], (16, 128)).astype(BF16)
            grad_z = jnp.dot(
                jnp.concatenate(
                    [
                        flat,
                        eye * jnp.concatenate([low_line] * 8, axis=0),
                        eye * jnp.concatenate([high_line] * 8, axis=0),
                    ],
                    axis=1,
                ),
                z_table,
                preferred_element_type=F32,
            )
            pair = slice(c // 2 * 16, c // 2 * 16 + 16)
            grad_y = jnp.dot(
                y_tables[c % 2],
                jnp.concatenate([flat, y_lows[pair], y_highs[pair]], axis=0),
                preferred_element_type=F32,
            )
            next_slope = [(nodes[c + 2][k] - nodes[c + 1][k]) * 0.125 for k in range(3)]
            wide = [before if c == 0 else ref_in[x0 + c * 8 - 1].astype(F32)]
            wide += [block[s].astype(F32) for s in range(8)]
            wide += [after if c == cells - 1 else ref_in[x0 + c * 8 + 8].astype(F32)]
            for s in range(8):
                if s == 0:
                    value = [nodes[c + 1][k] - 3.5 * slope[k] for k in range(3)]
                elif s == 4:
                    slope = next_slope
                    value = [nodes[c + 1][k] + 0.5 * slope[k] for k in range(3)]
                else:
                    value = [value[k] + slope[k] for k in range(3)]
                line = c * 8 + s
                rows_s = slice(s * 16, s * 16 + 16)
                total = def_in[x0 + line].astype(F32) - wide[s + 1]
                total = total - (wide[s + 2] - wide[s]) * value[0]
                total = total - grad_y[rows_s] * value[1]
                total = total - grad_z[rows_s] * value[2]
                out_buf[x0 + line] = total.astype(BF16)
        send(step).start()
        return 0

    lax.fori_loop(0, steps, body, 0)
    for step in range(steps):
        send(step).wait()


def solution(mesh):
    gx, gy, gz = (mesh.shape[a] for a in ("gx", "gy", "gz"))

    def on_device(ref_image, def_image, displacement):
        sizex, sizey, sizez = ref_image.shape
        rows = sizex // 8
        weights, table = solve_tables(gx, rows)
        chunk = 64
        disp = jnp.transpose(displacement, (0, 2, 3, 1))
        coarse_shape = (2, rows, 128)
        z_rows = 3 * rows + 32
        y_rows = 3 * rows + sizex
        params = pltpu.CompilerParams(vmem_limit_bytes=VMEM_BYTES)
        coarse, up, down, y_high, y_low = pl.pallas_call(
            lambda *refs: bin_kernel(chunk, *refs),
            name="bin_and_pack",
            in_specs=[HBM] * 3,
            out_specs=[VMEM] * 5,
            out_shape=[
                jax.ShapeDtypeStruct(coarse_shape, F32),
                jax.ShapeDtypeStruct((z_rows, 128), BF16),
                jax.ShapeDtypeStruct((z_rows, 128), BF16),
                jax.ShapeDtypeStruct((sizex, 128), BF16),
                jax.ShapeDtypeStruct((sizex, 128), BF16),
            ],
            scratch_shapes=[
                pltpu.VMEM(ref_image.shape, BF16),
                pltpu.VMEM(def_image.shape, BF16),
                pltpu.VMEM(disp.shape, F32),
                pltpu.VMEM((2, 2, rows, 128), F32),
                pltpu.VMEM((2, 32, 128), F32),
                pltpu.SemaphoreType.DMA((2, sizex // chunk)),
                pltpu.SemaphoreType.DMA,
            ],
            compiler_params=params,
        )(ref_image, def_image, disp)
        z_low = lax.ppermute(up, "gz", [(i, (i + 1) % gz) for i in range(gz)])
        z_high = lax.ppermute(down, "gz", [((i + 1) % gz, i) for i in range(gz)])
        coarse, down, up = pl.pallas_call(
            lambda *refs: z_kernel(gz, *refs),
            name="extend_along_z",
            in_specs=[VMEM] * 5,
            out_specs=[VMEM] * 3,
            out_shape=[
                jax.ShapeDtypeStruct(coarse_shape, F32),
                jax.ShapeDtypeStruct((y_rows, 128), BF16),
                jax.ShapeDtypeStruct((y_rows, 128), BF16),
            ],
            compiler_params=params,
        )(coarse, z_low, z_high, y_high, y_low)
        above = lax.ppermute(down, "gy", [(i + 1, i) for i in range(gy - 1)])
        below = lax.ppermute(up, "gy", [(i, i + 1) for i in range(gy - 1)])
        slabs, rhs, disp = pl.pallas_call(
            rhs_kernel,
            name="right_hand_sides",
            in_specs=[VMEM] * 5,
            out_specs=[VMEM] * 3,
            out_shape=[
                jax.ShapeDtypeStruct((gx, SLAB, 128), BF16),
                jax.ShapeDtypeStruct((3, rows, 128), F32),
                jax.ShapeDtypeStruct((3, rows, 128), F32),
            ],
            compiler_params=params,
        )(coarse, above, below, ref_image, jnp.asarray(weights))
        slabs = lax.all_to_all(slabs, "gx", 0, 0, tiled=True)
        new, residual = pl.pallas_call(
            fine_kernel,
            name="solve_and_residual",
            in_specs=[VMEM] * 11,
            out_specs=[VMEM, HBM],
            out_shape=[
                jax.ShapeDtypeStruct((3, 2, 16, rows), F32),
                jax.ShapeDtypeStruct(ref_image.shape, BF16),
            ],
            scratch_shapes=[
                pltpu.VMEM((gx, 32, 128), F32),
                pltpu.VMEM((16 * 3 * EXT, 128), F32),
                pltpu.VMEM((2, rows, 128), F32),
                pltpu.VMEM(ref_image.shape, BF16),
                pltpu.SemaphoreType.DMA((rows // 4,)),
            ],
            compiler_params=params,
        )(
            slabs, rhs, disp, jnp.asarray(table), jnp.asarray(prolong_table(sizey, sizez)),
            z_low, z_high, above, below, ref_image, def_image,
        )
        return jnp.transpose(new, (0, 3, 1, 2)), residual

    return jax.shard_map(
        on_device,
        mesh=mesh,
        in_specs=(P("gx", "gy", "gz"), P("gx", "gy", "gz"), P(None, "gx", "gy", "gz")),
        out_specs=(P(None, "gx", "gy", "gz"), P("gx", "gy", "gz")),
        check_vma=False,
    )
```

time: 59.3 us -> 52.1 us (0.88)
  Pallas kernels: 14.7 us -> 7.6 us
  waiting for transfers between devices: 18.5 us -> 11.4 us
  blocking collectives: 14.7 us -> 17.3 us
  starting transfers between devices: 8.9 us -> 11.5 us
  local copies, waits for them, and re-layouts: 1.23 us -> 3.27 us
    ppermute x2, waiting for transfers between devices: 13.4 us -> 6.47 us  [the longest x1 6.47 us: on_device(): above = lax.ppermute(down, 'gy', [(i + 1, i) for i in range(gy - 1)])]
    pallas_call x2, Pallas kernels: 8.92 us -> 5.39 us  [the longest x1 5.02 us: on_device(): pl.pallas_call(fine_kernel, name='solve_and_residual', in_specs=[VMEM] *...]
    all_to_all x1, blocking collectives: 14.7 us -> 17.3 us  [on_device(): slabs = lax.all_to_all(slabs, 'gx', 0, 0, tiled=True)]
    ppermute x2, starting transfers between devices: 7.16 us -> 9.74 us  [the longest x1 8.46 us: on_device(): below = lax.ppermute(up, 'gy', [(i, i + 1) for i in range(gy - 1)])]
    unnamed x8 -> x16, local copies, waits for them, and re-layouts: 1.23 us -> 3.27 us
    pallas_call x1, Pallas kernels: 4 us -> 2.05 us  [on_device(): pl.pallas_call(lambda *refs: bin_kernel(chunk, *refs), name='bin_and_pack...]
    pallas_call x1, Pallas kernels: 1.75 us -> 0.16 us  [on_device(): pl.pallas_call(lambda *refs: z_kernel(gz, *refs), name='extend_along_z',...]
  transfers between devices with their start and end apart: 4 -> 4, of which waited for: 4 -> 3; matrix products, arithmetic and copies ran while one was open for 0% -> 0% of each run, Pallas kernels for 0% -> 0%
where the time goes in v2:
time: 52.1 us; the launch traced here: 51.8 us
  blocking collectives  17.3 us (33%)
  starting transfers between devices  11.5 us (22%)
  waiting for transfers between devices  11.4 us (22%)
  Pallas kernels  7.6 us (15%)
  local copies, waits for them, and re-layouts  3.27 us (6%)
  between operations  0.72 us (1%)
    all_to_all x1, blocking collectives, on_device(): slabs = lax.all_to_all(slabs, 'gx', 0, 0, tiled=True)  17.3 us
    ppermute x1, starting transfers between devices, on_device(): below = lax.ppermute(up, 'gy', [(i, i + 1) for i in range(gy - 1)])  8.46 us
    ppermute x1, waiting for transfers between devices, on_device(): above = lax.ppermute(down, 'gy', [(i + 1, i) for i in range(gy - 1)])  6.47 us
    pallas_call x1, Pallas kernels, on_device(): pl.pallas_call(fine_kernel, name='solve_and_residual', in_specs=[VMEM] *...  5.02 us
    ppermute x1, waiting for transfers between devices, on_device(): z_high = lax.ppermute(down, 'gz', [((i + 1) % gz, i) for i in range(gz)])  3.33 us
    unnamed x16, local copies, waits for them, and re-layouts  3.27 us
    pallas_call x1, Pallas kernels, on_device(): pl.pallas_call(lambda *refs: bin_kernel(chunk, *refs), name='bin_and_pack...  2.05 us
    ppermute x1, starting transfers between devices, on_device(): z_high = lax.ppermute(down, 'gz', [((i + 1) % gz, i) for i in range(gz)])  1.73 us
  transfers between devices with their start and end apart: 4, of which 3 were waited for; matrix products, arithmetic and copies ran while one was open for 0% of the time, Pallas kernels for 0%

profile of v2, /device:TPU:6, one launch (start us, length us, event | category | flops | bytes accessed | tf_op | source)
XLA Modules:
  0.0 51.8 jit_solution(2126300994611783596)
XLA Ops:
  0.6 0.0 copy-start
  0.6 1.2 %copy-done = bf16[256,16,128]{2,1,0:T(8,128)(2,1)S(1)} copy-done((bf16[256,16,128]{2,1,0:T(8,128)(2,1)S(1)}, bf16[256,16,128]{2,1,0:T(8,128)(2,1)}, u32[]{:S(2)}) %copy-start) | copy-done | bytes 1048600
  1.9 0.0 copy-start.2
  1.9 1.2 %copy-done.2 = bf16[256,16,128]{2,1,0:T(8,128)(2,1)S(1)} copy-done((bf16[256,16,128]{2,1,0:T(8,128)(2,1)S(1)}, bf16[256,16,128]{2,1,0:T(8,128)(2,1)}, u32[]{:S(2)}) %copy-start.2) | copy-done | bytes 1048600
  3.1 0.0 copy-start.7
  3.1 0.8 %copy-done.7 = f32[3,32,2,16]{1,3,2,0:T(8,128)S(1)} copy-done((f32[3,32,2,16]{1,3,2,0:T(8,128)S(1)}, f32[3,32,2,16]{1,3,2,0:T(8,128)}, u32[]{:S(2)}) %copy-start.7) | copy-done | bytes 12312
  3.9 0.0 copy-start.1
  3.9 0.0 copy-start.6
  3.9 2.1 %bin_and_pack.1 = (f32[2,32,128]{2,1,0:T(8,128)S(1)}, bf16[128,128]{1,0:T(8,128)(2,1)S(1)}, bf16[128,128]{1,0:T(8,128)(2,1)S(1)}, bf16[256,128]{1,0:T(8,128)(2,1)S(1)}, bf16[256,128]{1,0:T(8,128)(2,1)S(1)}) custom-call(bf16[256,16,128]{2,1,0:T(8,128)(2,1)S(1)} %copy-done, bf16[256,16,128]{2,1,0:T(8,128)(2,1)S(1)} %copy-done.2, f32[3,2,16,32]{3,2,1,0:T(8,128)S(1)} %bitcast.2), custom_call_target="tpu_custom_call" | custom-call | tf_op jit(solution)/shard_map/bin_and_pack/pallas_call | solution.py:452
  5.9 0.0 copy-start.3
  6.0 0.0 collective-permute-start
  6.0 1.7 %collective-permute-start.1 = (bf16[128,128]{1,0:T(8,128)(2,1)S(1)}, bf16[128,128]{1,0:T(8,128)(2,1)S(1)}, u32[]{:S(2)}, u32[]{:S(2)}) collective-permute-start(bf16[128,128]{1,0:T(8,128)(2,1)S(1)} %get-tuple-element.17), channel_id=1, source_target_pairs={{1,0},{2,1},{3,2},{4,3},{5,4},{6,5},{7,6},{0,7},{9,8},{10,9},{11,1... | collective-permute-start | bytes 98312 | tf_op jit(solution)/shard_map/ppermute | solution.py:476
  7.7 1.6 %collective-permute-done.refs_1_.z_low_in = bf16[128,128]{1,0:T(8,128)(2,1)S(1)} collective-permute-done((bf16[128,128]{1,0:T(8,128)(2,1)S(1)}, bf16[128,128]{1,0:T(8,128)(2,1)S(1)}, u32[]{:S(2)}, u32[]{:S(2)}) %collective-permute-start) | collective-permute-done | bytes 32800 | tf_op jit(solution)/shard_map/ppermute | solution.py:475
  9.3 3.3 %collective-permute-done.1.refs_2_.z_high_in = bf16[128,128]{1,0:T(8,128)(2,1)S(1)} collective-permute-done((bf16[128,128]{1,0:T(8,128)(2,1)S(1)}, bf16[128,128]{1,0:T(8,128)(2,1)S(1)}, u32[]{:S(2)}, u32[]{:S(2)}) %collective-permute-start.1) | collective-permute-done | bytes 32800 | tf_op jit(solution)/shard_map/ppermute | solution.py:476
  12.6 0.2 extend_along_z.1
  12.8 1.3 %collective-permute-start.2 = (bf16[352,128]{1,0:T(8,128)(2,1)S(1)}, bf16[352,128]{1,0:T(8,128)(2,1)S(1)}, u32[]{:S(2)}, u32[]{:S(2)}) collective-permute-start(bf16[352,128]{1,0:T(8,128)(2,1)S(1)} %get-tuple-element.21), channel_id=1, source_target_pairs={{8,0},{16,8},{24,16},{9,1},{17,9},{25,17},{10,2},{18,10},{26,18},{... | collective-permute-start | bytes 270344 | tf_op jit(solution)/shard_map/ppermute | solution.py:489
  14.1 8.5 %collective-permute-start.3 = (bf16[352,128]{1,0:T(8,128)(2,1)S(1)}, bf16[352,128]{1,0:T(8,128)(2,1)S(1)}, u32[]{:S(2)}, u32[]{:S(2)}) collective-permute-start(bf16[352,128]{1,0:T(8,128)(2,1)S(1)} %get-tuple-element.22), channel_id=1, source_target_pairs={{0,8},{8,16},{16,24},{1,9},{9,17},{17,25},{2,10},{10,18},{18,26},{... | collective-permute-start | bytes 270344 | tf_op jit(solution)/shard_map/ppermute | solution.py:490
  22.6 6.5 %collective-permute-done.2.above_in = bf16[352,128]{1,0:T(8,128)(2,1)S(1)} collective-permute-done((bf16[352,128]{1,0:T(8,128)(2,1)S(1)}, bf16[352,128]{1,0:T(8,128)(2,1)S(1)}, u32[]{:S(2)}, u32[]{:S(2)}) %collective-permute-start.2) | collective-permute-done | bytes 90144 | tf_op jit(solution)/shard_map/ppermute | solution.py:489
  29.0 0.0 collective-permute-done.3.below_in
  29.0 0.0 copy-done.1
  29.0 0.0 copy-done.6
  29.0 0.0 copy-start.4
  29.0 0.4 right_hand_sides.1
  29.4 0.0 copy-start.5
  29.4 17.3 %all_to_all.5.slab_in = bf16[16,48,128]{2,1,0:T(8,128)(2,1)S(1)} all-to-all(bf16[16,48,128]{2,1,0:T(8,128)(2,1)S(1)} %get-tuple-element.23), channel_id=1, replica_groups=mesh['gx'=16,'gy'=4,'gz'=8] {'gx'}, dimensions={0} | all-to-all | bytes 393216 | tf_op jit(solution)/shard_map/all_to_all | solution.py:503
  46.8 0.0 copy-done.3
  46.8 0.0 copy-done.4
  46.8 0.0 copy-done.5
  46.8 5.0 %solve_and_residual.1 = (f32[3,2,16,32]{3,2,1,0:T(8,128)}, bf16[256,16,128]{2,1,0:T(8,128)(2,1)}) custom-call(bf16[16,48,128]{2,1,0:T(8,128)(2,1)S(1)} %all_to_all.5.slab_in, f32[3,32,128]{2,1,0:T(8,128)S(1)} %get-tuple-element.24.rhs_in, f32[3,32,128]{2,1,0:T(8,128)S(1)} %get-tuple-element.25.disp_in, f32[16,40,80]{2,1,0:T(8,128)S(1)} %copy-done.5, ...), custom_call_target="tpu_custom_call" | custom-call | tf_op jit(solution)/shard_map/solve_and_residual/pallas_call | solution.py:504
Async XLA Ops:
  0.6 1.2 %copy-start = (bf16[256,16,128]{2,1,0:T(8,128)(2,1)S(1)}, bf16[256,16,128]{2,1,0:T(8,128)(2,1)}, u32[]{:S(2)}) copy-start(bf16[256,16,128]{2,1,0:T(8,128)(2,1)} %ref_in.3) | copy-start | bytes 3145732
  1.9 1.2 %copy-start.2 = (bf16[256,16,128]{2,1,0:T(8,128)(2,1)S(1)}, bf16[256,16,128]{2,1,0:T(8,128)(2,1)}, u32[]{:S(2)}) copy-start(bf16[256,16,128]{2,1,0:T(8,128)(2,1)} %def_in.1) | copy-start | bytes 3145732
  3.1 0.8 %copy-start.7 = (f32[3,32,2,16]{1,3,2,0:T(8,128)S(1)}, f32[3,32,2,16]{1,3,2,0:T(8,128)}, u32[]{:S(2)}) copy-start(f32[3,32,2,16]{1,3,2,0:T(8,128)} %param.8) | copy-start | bytes 36868
  3.9 25.1 %copy-start.1 = (bf16[256,16,128]{2,1,0:T(8,128)(2,1)S(1)}, bf16[256,16,128]{2,1,0:T(8,128)(2,1)}, u32[]{:S(2)}) copy-start(bf16[256,16,128]{2,1,0:T(8,128)(2,1)} %ref_in.3) | copy-start | bytes 3145732
  3.9 25.2 %copy-start.6 = (f32[16,8,32]{2,1,0:T(8,128)S(1)}, f32[16,8,32]{2,1,0:T(8,128)}, u32[]{:S(2)}) copy-start(f32[16,8,32]{2,1,0:T(8,128)} %constant.6.clone.weights_in) | copy-start | bytes 49156
  5.9 40.8 %copy-start.3 = (bf16[256,16,128]{2,1,0:T(8,128)(2,1)S(1)}, bf16[256,16,128]{2,1,0:T(8,128)(2,1)}, u32[]{:S(2)}) copy-start(bf16[256,16,128]{2,1,0:T(8,128)(2,1)} %def_in.1) | copy-start | bytes 3145732
  6.0 3.4 %collective-permute-start = (bf16[128,128]{1,0:T(8,128)(2,1)S(1)}, bf16[128,128]{1,0:T(8,128)(2,1)S(1)}, u32[]{:S(2)}, u32[]{:S(2)}) collective-permute-start(bf16[128,128]{1,0:T(8,128)(2,1)S(1)} %get-tuple-element.16), channel_id=1, source_target_pairs={{0,1},{1,2},{2,3},{3,4},{4,5},{5,6},{6,7},{7,0},{8,9},{9,10},{10,1... | collective-permute-start | bytes 98312 | tf_op jit(solution)/shard_map/ppermute | solution.py:475
  6.0 6.7 %collective-permute-start.1 = (bf16[128,128]{1,0:T(8,128)(2,1)S(1)}, bf16[128,128]{1,0:T(8,128)(2,1)S(1)}, u32[]{:S(2)}, u32[]{:S(2)}) collective-permute-start(bf16[128,128]{1,0:T(8,128)(2,1)S(1)} %get-tuple-element.17), channel_id=1, source_target_pairs={{1,0},{2,1},{3,2},{4,3},{5,4},{6,5},{7,6},{0,7},{9,8},{10,9},{11,1... | collective-permute-start | bytes 98312 | tf_op jit(solution)/shard_map/ppermute | solution.py:476
  12.8 16.2 %collective-permute-start.2 = (bf16[352,128]{1,0:T(8,128)(2,1)S(1)}, bf16[352,128]{1,0:T(8,128)(2,1)S(1)}, u32[]{:S(2)}, u32[]{:S(2)}) collective-permute-start(bf16[352,128]{1,0:T(8,128)(2,1)S(1)} %get-tuple-element.21), channel_id=1, source_target_pairs={{8,0},{16,8},{24,16},{9,1},{17,9},{25,17},{10,2},{18,10},{26,18},{... | collective-permute-start | bytes 270344 | tf_op jit(solution)/shard_map/ppermute | solution.py:489
  14.1 14.9 %collective-permute-start.3 = (bf16[352,128]{1,0:T(8,128)(2,1)S(1)}, bf16[352,128]{1,0:T(8,128)(2,1)S(1)}, u32[]{:S(2)}, u32[]{:S(2)}) collective-permute-start(bf16[352,128]{1,0:T(8,128)(2,1)S(1)} %get-tuple-element.22), channel_id=1, source_target_pairs={{0,8},{8,16},{16,24},{1,9},{9,17},{17,25},{2,10},{10,18},{18,26},{... | collective-permute-start | bytes 270344 | tf_op jit(solution)/shard_map/ppermute | solution.py:490
  29.0 17.7 %copy-start.4 = (bf16[128,2048]{1,0:T(8,128)(2,1)S(1)}, bf16[128,2048]{1,0:T(8,128)(2,1)}, u32[]{:S(2)}) copy-start(bf16[128,2048]{1,0:T(8,128)(2,1)} %constant.8.clone.prolong_in) | copy-start | bytes 1572868
  29.4 17.3 %copy-start.5 = (f32[16,40,80]{2,1,0:T(8,128)S(1)}, f32[16,40,80]{2,1,0:T(8,128)}, u32[]{:S(2)}) copy-start(f32[16,40,80]{2,1,0:T(8,128)} %constant.7.clone.table_in) | copy-start | bytes 614404

commit v3 on v2

--- a/solution.py
+++ b/solution.py
@@ -15,6 +15,7 @@
 BF16 = jnp.bfloat16
 SLAB = 48
 VMEM_BYTES = 16 * 2**20
+FIRST_VMEM_BYTES = 54400 * 2**10
 EXT = 40
 
 
@@ -202,7 +203,7 @@
 
 
 def rhs_kernel(
-    coarse_in, above_in, below_in, ref_in, weights_in,
+    coarse_in, above_in, below_in, ref_in, weights_in, _,
     slab_out, rhs_out, disp_out,
 ):
     rows = coarse_in.shape[1]
@@ -267,17 +268,70 @@
         slab_out[q, 16:48, :] = jnp.where(me > q, to_below, to_above)
 
 
+def gradient_kernel(
+    z_low_in, z_high_in, ref_in, slopes, z_faces
+):
+    sizex = ref_in.shape[0]
+    rows = sizex // 8
+    me_z = lax.axis_index("gz")
+    last_z = lax.axis_size("gz") - 1
+    z_faces[0] = jnp.where(me_z > 0, z_low_in[3 * rows :, :].astype(F32), 0.0)
+    z_faces[1] = jnp.where(me_z < last_z, z_high_in[3 * rows :, :].astype(F32), 0.0)
+    eye = jnp.where(iota((128, 128), 0) == iota((128, 128), 1), 1.0, 0.0).astype(BF16)
+    z_from, z_to = iota((384, 128), 0), iota((384, 128), 1)
+    z_table = jnp.where((z_from == z_to + 1) & (z_from < 128), 1.0, 0.0)
+    z_table -= jnp.where(z_from + 1 == z_to, 1.0, 0.0)
+    z_table -= jnp.where((z_from >= 128) & (z_from < 256) & (z_to == 0), 1.0, 0.0)
+    z_table += jnp.where((z_from >= 256) & (z_to == 127), 1.0, 0.0)
+    z_table = z_table.astype(BF16)
+    y_to, y_from = iota((128, 128), 0), iota((128, 128), 1)
+    y_table = jnp.where((y_from == y_to + 1) & (y_to % 16 != 15), 1.0, 0.0)
+    y_table -= jnp.where((y_from + 1 == y_to) & (y_to % 16 != 0), 1.0, 0.0)
+    y_table = y_table.astype(BF16)
+    cells = 4
+    steps = rows // cells
+
+    def body(step, _):
+        x0 = step * (cells * 8)
+        for c in range(cells):
+            here = step * cells + c
+            block = ref_in[pl.ds(x0 + c * 8, 8)]
+            flat = block.reshape(128, 128)
+            low_line = jnp.broadcast_to(z_faces[0, pl.ds(here, 1), :], (16, 128)).astype(BF16)
+            high_line = jnp.broadcast_to(z_faces[1, pl.ds(here, 1), :], (16, 128)).astype(BF16)
+            grad_z = jnp.dot(
+                jnp.concatenate(
+                    [
+                        flat,
+                        eye * jnp.concatenate([low_line] * 8, axis=0),
+                        eye * jnp.concatenate([high_line] * 8, axis=0),
+                    ],
+                    axis=1,
+                ),
+                z_table,
+                preferred_element_type=F32,
+            )
+            grad_y = jnp.dot(y_table, flat, preferred_element_type=F32)
+            planes = pl.ds(x0 + c * 8, 8)
+            slopes[0, planes] = grad_y.reshape(8, 16, 128)
+            slopes[1, planes] = grad_z.reshape(8, 16, 128)
+        return 0
+
+    lax.fori_loop(0, steps, body, 0)
+
+
 def fine_kernel(
-    slab_in, rhs_in, disp_in, table_in, prolong_in, z_low_in, z_high_in, above_in, below_in,
-    ref_in, def_in,
+    slab_in, rhs_in, disp_in, table_in, prolong_in, slopes, above_in, below_in, ref_in, def_in,
     disp_out, out_hbm,
-    lines, field, z_faces, out_buf, sems,
+    lines, field, out_buf, sems,
 ):
+    cells = 4
+    sizex = ref_in.shape[0]
+    steps = sizex // (8 * cells)
+
     devices = slab_in.shape[0]
     rows = rhs_in.shape[1]
     me = lax.axis_index("gx")
-    me_z = lax.axis_index("gz")
-    last_z = lax.axis_size("gz") - 1
     height = 3 * EXT
     lines[...] = slab_in[:, 16:48, :].astype(F32)
     lane = iota((devices, 128), 1)
@@ -340,30 +394,11 @@
         for y in range(2):
             disp_out[k, y] = placed[16 * y : 16 * y + 16, k * rows : (k + 1) * rows]
 
-    z_faces[0] = jnp.where(me_z > 0, z_low_in[3 * rows :, :].astype(F32), 0.0)
-    z_faces[1] = jnp.where(me_z < last_z, z_high_in[3 * rows :, :].astype(F32), 0.0)
-    eye = jnp.where(iota((128, 128), 0) == iota((128, 128), 1), 1.0, 0.0).astype(BF16)
-    z_from, z_to = iota((384, 128), 0), iota((384, 128), 1)
-    z_table = jnp.where((z_from == z_to + 1) & (z_from < 128), 1.0, 0.0)
-    z_table -= jnp.where(z_from + 1 == z_to, 1.0, 0.0)
-    z_table -= jnp.where((z_from >= 128) & (z_from < 256) & (z_to == 0), 1.0, 0.0)
-    z_table += jnp.where((z_from >= 256) & (z_to == 127), 1.0, 0.0)
-    z_table = z_table.astype(BF16)
-    y_to, y_from = iota((128, 160), 0), iota((128, 160), 1)
-    y_tables = []
-    for half in range(2):
-        low_at = 128 + 8 * half + y_to // 16
-        plus = jnp.where(y_to % 16 == 15, low_at + 16, y_to + 1)
-        minus = jnp.where(y_to % 16 == 0, low_at, y_to - 1)
-        y_table = jnp.where(y_from == plus, 1.0, 0.0) - jnp.where(y_from == minus, 1.0, 0.0)
-        y_tables.append(y_table.astype(BF16))
     x_low = slab_in[jnp.maximum(me - 1, 0), 0:16, :].astype(F32)
     x_low = jnp.where(me > 0, x_low, 0.0)
     x_high = slab_in[jnp.minimum(me + 1, devices - 1), 0:16, :].astype(F32)
     x_high = jnp.where(me < devices - 1, x_high, 0.0)
-    cells = 4
-    sizex = ref_in.shape[0]
-    steps = rows // cells
+    row = iota((16, 128), 0)
 
     def send(step):
         planes = pl.ds(step * cells * 8, cells * 8)
@@ -371,13 +406,13 @@
 
     def body(step, _):
         x0 = step * (cells * 8)
+        y_rows = pl.ds(pl.multiple_of(3 * rows + x0, 32), cells * 8)
+        y_lows = below_in[y_rows, :].astype(F32)
+        y_highs = above_in[y_rows, :].astype(F32)
         before = ref_in[jnp.maximum(x0 - 1, 0)].astype(F32)
         before = jnp.where(step > 0, before, x_low)
         after = ref_in[jnp.minimum(x0 + cells * 8, sizex - 1)].astype(F32)
         after = jnp.where(step < steps - 1, after, x_high)
-        y_rows = pl.ds(pl.multiple_of(3 * rows + x0, 32), cells * 8)
-        y_lows = below_in[y_rows, :]
-        y_highs = above_in[y_rows, :]
         index_low = jnp.where(step > 0, step * cells - 1, rows)
         index_high = jnp.where(step < steps - 1, step * cells + cells, rows + 1)
         indices = [index_low] + [step * cells + c for c in range(cells)] + [index_high]
@@ -386,30 +421,8 @@
         ]
         slope = [(nodes[1][k] - nodes[0][k]) * 0.125 for k in range(3)]
         for c in range(cells):
-            here = step * cells + c
+            next_slope = [(nodes[c + 2][k] - nodes[c + 1][k]) * 0.125 for k in range(3)]
             block = ref_in[pl.ds(x0 + c * 8, 8)]
-            flat = block.reshape(128, 128)
-            low_line = jnp.broadcast_to(z_faces[0, pl.ds(here, 1), :], (16, 128)).astype(BF16)
-            high_line = jnp.broadcast_to(z_faces[1, pl.ds(here, 1), :], (16, 128)).astype(BF16)
-            grad_z = jnp.dot(
-                jnp.concatenate(
-                    [
-                        flat,
-                        eye * jnp.concatenate([low_line] * 8, axis=0),
-                        eye * jnp.concatenate([high_line] * 8, axis=0),
-                    ],
-                    axis=1,
-                ),
-                z_table,
-                preferred_element_type=F32,
-            )
-            pair = slice(c // 2 * 16, c // 2 * 16 + 16)
-            grad_y = jnp.dot(
-                y_tables[c % 2],
-                jnp.concatenate([flat, y_lows[pair], y_highs[pair]], axis=0),
-                preferred_element_type=F32,
-            )
-            next_slope = [(nodes[c + 2][k] - nodes[c + 1][k]) * 0.125 for k in range(3)]
             wide = [before if c == 0 else ref_in[x0 + c * 8 - 1].astype(F32)]
             wide += [block[s].astype(F32) for s in range(8)]
             wide += [after if c == cells - 1 else ref_in[x0 + c * 8 + 8].astype(F32)]
@@ -421,13 +434,15 @@
                     value = [nodes[c + 1][k] + 0.5 * slope[k] for k in range(3)]
                 else:
                     value = [value[k] + slope[k] for k in range(3)]
+                x = x0 + c * 8 + s
+                total = def_in[x].astype(F32) - wide[s + 1]
+                total = total - (wide[s + 2] - wide[s]) * value[0]
                 line = c * 8 + s
-                rows_s = slice(s * 16, s * 16 + 16)
-                total = def_in[x0 + line].astype(F32) - wide[s + 1]
-                total = total - (wide[s + 2] - wide[s]) * value[0]
-                total = total - grad_y[rows_s] * value[1]
-                total = total - grad_z[rows_s] * value[2]
-                out_buf[x0 + line] = total.astype(BF16)
+                y_edge = jnp.where(row == 0, -y_lows[line : line + 1], 0.0)
+                y_edge = jnp.where(row == 15, y_highs[line : line + 1], y_edge)
+                total = total - (slopes[0, x] + y_edge) * value[1]
+                total = total - slopes[1, x] * value[2]
+                out_buf[x] = total.astype(BF16)
         send(step).start()
         return 0
 
@@ -449,6 +464,7 @@
         z_rows = 3 * rows + 32
         y_rows = 3 * rows + sizex
         params = pltpu.CompilerParams(vmem_limit_bytes=VMEM_BYTES)
+        first_params = pltpu.CompilerParams(vmem_limit_bytes=FIRST_VMEM_BYTES)
         coarse, up, down, y_high, y_low = pl.pallas_call(
             lambda *refs: bin_kernel(chunk, *refs),
             name="bin_and_pack",
@@ -470,7 +486,7 @@
                 pltpu.SemaphoreType.DMA((2, sizex // chunk)),
                 pltpu.SemaphoreType.DMA,
             ],
-            compiler_params=params,
+            compiler_params=first_params,
         )(ref_image, def_image, disp)
         z_low = lax.ppermute(up, "gz", [(i, (i + 1) % gz) for i in range(gz)])
         z_high = lax.ppermute(down, "gz", [((i + 1) % gz, i) for i in range(gz)])
@@ -488,10 +504,21 @@
         )(coarse, z_low, z_high, y_high, y_low)
         above = lax.ppermute(down, "gy", [(i + 1, i) for i in range(gy - 1)])
         below = lax.ppermute(up, "gy", [(i, i + 1) for i in range(gy - 1)])
+        slopes_shape = (2,) + ref_image.shape
+        chunks = rows // 4
+        slopes = pl.pallas_call(
+            gradient_kernel,
+            name="gradients",
+            in_specs=[VMEM] * 3,
+            out_specs=VMEM,
+            out_shape=jax.ShapeDtypeStruct(slopes_shape, F32),
+            scratch_shapes=[pltpu.VMEM((2, rows, 128), F32)],
+            compiler_params=params,
+        )(z_low, z_high, ref_image)
         slabs, rhs, disp = pl.pallas_call(
             rhs_kernel,
             name="right_hand_sides",
-            in_specs=[VMEM] * 5,
+            in_specs=[VMEM] * 5 + [pl.BlockSpec(memory_space=pl.ANY)],
             out_specs=[VMEM] * 3,
             out_shape=[
                 jax.ShapeDtypeStruct((gx, SLAB, 128), BF16),
@@ -499,12 +526,12 @@
                 jax.ShapeDtypeStruct((3, rows, 128), F32),
             ],
             compiler_params=params,
-        )(coarse, above, below, ref_image, jnp.asarray(weights))
+        )(coarse, above, below, ref_image, jnp.asarray(weights), slopes)
         slabs = lax.all_to_all(slabs, "gx", 0, 0, tiled=True)
         new, residual = pl.pallas_call(
             fine_kernel,
             name="solve_and_residual",
-            in_specs=[VMEM] * 11,
+            in_specs=[VMEM] * 10,
             out_specs=[VMEM, HBM],
             out_shape=[
                 jax.ShapeDtypeStruct((3, 2, 16, rows), F32),
@@ -513,14 +540,13 @@
             scratch_shapes=[
                 pltpu.VMEM((gx, 32, 128), F32),
                 pltpu.VMEM((16 * 3 * EXT, 128), F32),
-                pltpu.VMEM((2, rows, 128), F32),
                 pltpu.VMEM(ref_image.shape, BF16),
-                pltpu.SemaphoreType.DMA((rows // 4,)),
+                pltpu.SemaphoreType.DMA((chunks,)),
             ],
             compiler_params=params,
         )(
             slabs, rhs, disp, jnp.asarray(table), jnp.asarray(prolong_table(sizey, sizez)),
-            z_low, z_high, above, below, ref_image, def_image,
+            slopes, above, below, ref_image, def_image,
         )
         return jnp.transpose(new, (0, 3, 1, 2)), residual
 

time: 52.1 us -> 48.9 us (0.939)
  waiting for transfers between devices: 11.4 us -> 7.75 us
  Pallas kernels: 7.6 us -> 9.38 us
  local copies, waits for them, and re-layouts: 3.27 us -> 2.07 us
    ppermute x1, waiting for transfers between devices: 6.47 us -> 2.83 us  [on_device(): above = lax.ppermute(down, 'gy', [(i + 1, i) for i in range(gy - 1)])]
    pallas_call x1 -> x2, Pallas kernels: 0.37 us -> 2.74 us  [the longest x1 2.37 us: on_device(): pl.pallas_call(gradient_kernel, name='gradients', in_specs=[VMEM] * 3, ou...]
    pallas_call x1, Pallas kernels: 5.02 us -> 3.67 us  [on_device(): pl.pallas_call(fine_kernel, name='solve_and_residual', in_specs=[VMEM] *...]
    unnamed x16 -> x12, local copies, waits for them, and re-layouts: 3.27 us -> 2.07 us
    pallas_call x1, Pallas kernels: 2.05 us -> 2.81 us  [on_device(): pl.pallas_call(lambda *refs: bin_kernel(chunk, *refs), name='bin_and_pack...]
  transfers between devices with their start and end apart: 4 -> 4, of which waited for: 3 -> 3; matrix products, arithmetic and copies ran while one was open for 0% -> 0% of each run, Pallas kernels for 0% -> 5%
where the time goes in v3:
time: 48.9 us; the launch traced here: 48.6 us
  blocking collectives  17.2 us (35%)
  starting transfers between devices  11.5 us (24%)
  Pallas kernels  9.38 us (19%)
  waiting for transfers between devices  7.75 us (16%)
  local copies, waits for them, and re-layouts  2.07 us (4%)
  between operations  0.73 us (1%)
    all_to_all x1, blocking collectives, on_device(): slabs = lax.all_to_all(slabs, 'gx', 0, 0, tiled=True)  17.2 us
    ppermute x1, starting transfers between devices, on_device(): below = lax.ppermute(up, 'gy', [(i, i + 1) for i in range(gy - 1)])  8.46 us
    pallas_call x1, Pallas kernels, on_device(): pl.pallas_call(fine_kernel, name='solve_and_residual', in_specs=[VMEM] *...  3.67 us
    ppermute x1, waiting for transfers between devices, on_device(): z_high = lax.ppermute(down, 'gz', [((i + 1) % gz, i) for i in range(gz)])  3.33 us
    ppermute x1, waiting for transfers between devices, on_device(): above = lax.ppermute(down, 'gy', [(i + 1, i) for i in range(gy - 1)])  2.83 us
    pallas_call x1, Pallas kernels, on_device(): pl.pallas_call(lambda *refs: bin_kernel(chunk, *refs), name='bin_and_pack...  2.81 us
    pallas_call x1, Pallas kernels, on_device(): pl.pallas_call(gradient_kernel, name='gradients', in_specs=[VMEM] * 3, ou...  2.37 us
    unnamed x12, local copies, waits for them, and re-layouts  2.07 us
  transfers between devices with their start and end apart: 4, of which 3 were waited for; matrix products, arithmetic and copies ran while one was open for 0% of the time, Pallas kernels for 5%

profile of v3, /device:TPU:6, one launch (start us, length us, event | category | flops | bytes accessed | tf_op | source)
XLA Modules:
  0.0 48.6 jit_solution(13992462588622490597)
XLA Ops:
  0.6 0.0 copy-start.4
  0.6 0.0 copy-start.5
  0.7 0.8 %copy-done.5 = f32[3,32,2,16]{1,3,2,0:T(8,128)S(1)} copy-done((f32[3,32,2,16]{1,3,2,0:T(8,128)S(1)}, f32[3,32,2,16]{1,3,2,0:T(8,128)}, u32[]{:S(2)}) %copy-start.5) | copy-done | bytes 12312
  1.5 2.8 %bin_and_pack.1 = (f32[2,32,128]{2,1,0:T(8,128)S(1)}, bf16[128,128]{1,0:T(8,128)(2,1)S(1)}, bf16[128,128]{1,0:T(8,128)(2,1)S(1)}, bf16[256,128]{1,0:T(8,128)(2,1)S(1)}, bf16[256,128]{1,0:T(8,128)(2,1)S(1)}) custom-call(bf16[256,16,128]{2,1,0:T(8,128)(2,1)} %ref_in.5, bf16[256,16,128]{2,1,0:T(8,128)(2,1)} %def_in.1, f32[3,2,16,32]{3,2,1,0:T(8,128)S(1)} %bitcast.2), custom_call_target="tpu_custom_call" | custom-call | tf_op jit(solution)/shard_map/bin_and_pack/pallas_call | solution.py:468
  4.3 0.0 collective-permute-start
  4.3 1.7 %collective-permute-start.1 = (bf16[128,128]{1,0:T(8,128)(2,1)S(1)}, bf16[128,128]{1,0:T(8,128)(2,1)S(1)}, u32[]{:S(2)}, u32[]{:S(2)}) collective-permute-start(bf16[128,128]{1,0:T(8,128)(2,1)S(1)} %get-tuple-element.17), channel_id=1, source_target_pairs={{1,0},{2,1},{3,2},{4,3},{5,4},{6,5},{7,6},{0,7},{9,8},{10,9},{11,1... | collective-permute-start | bytes 98312 | tf_op jit(solution)/shard_map/ppermute | solution.py:492
  6.1 1.6 %collective-permute-done.refs_1_.z_low_in = bf16[128,128]{1,0:T(8,128)(2,1)S(1)} collective-permute-done((bf16[128,128]{1,0:T(8,128)(2,1)S(1)}, bf16[128,128]{1,0:T(8,128)(2,1)S(1)}, u32[]{:S(2)}, u32[]{:S(2)}) %collective-permute-start) | collective-permute-done | bytes 32800 | tf_op jit(solution)/shard_map/ppermute | solution.py:491
  7.6 3.3 %collective-permute-done.1.refs_2_.z_high_in = bf16[128,128]{1,0:T(8,128)(2,1)S(1)} collective-permute-done((bf16[128,128]{1,0:T(8,128)(2,1)S(1)}, bf16[128,128]{1,0:T(8,128)(2,1)S(1)}, u32[]{:S(2)}, u32[]{:S(2)}) %collective-permute-start.1) | collective-permute-done | bytes 32800 | tf_op jit(solution)/shard_map/ppermute | solution.py:492
  11.0 0.2 extend_along_z.1
  11.1 1.3 %collective-permute-start.2 = (bf16[352,128]{1,0:T(8,128)(2,1)S(1)}, bf16[352,128]{1,0:T(8,128)(2,1)S(1)}, u32[]{:S(2)}, u32[]{:S(2)}) collective-permute-start(bf16[352,128]{1,0:T(8,128)(2,1)S(1)} %get-tuple-element.21), channel_id=1, source_target_pairs={{8,0},{16,8},{24,16},{9,1},{17,9},{25,17},{10,2},{18,10},{26,18},{... | collective-permute-start | bytes 270344 | tf_op jit(solution)/shard_map/ppermute | solution.py:505
  12.4 8.5 %collective-permute-start.3 = (bf16[352,128]{1,0:T(8,128)(2,1)S(1)}, bf16[352,128]{1,0:T(8,128)(2,1)S(1)}, u32[]{:S(2)}, u32[]{:S(2)}) collective-permute-start(bf16[352,128]{1,0:T(8,128)(2,1)S(1)} %get-tuple-element.22), channel_id=1, source_target_pairs={{0,8},{8,16},{16,24},{1,9},{9,17},{17,25},{2,10},{10,18},{18,26},{... | collective-permute-start | bytes 270344 | tf_op jit(solution)/shard_map/ppermute | solution.py:506
  20.9 0.0 copy-start
  20.9 1.2 %copy-done = bf16[256,16,128]{2,1,0:T(8,128)(2,1)S(1)} copy-done((bf16[256,16,128]{2,1,0:T(8,128)(2,1)S(1)}, bf16[256,16,128]{2,1,0:T(8,128)(2,1)}, u32[]{:S(2)}) %copy-start) | copy-done | bytes 1048600
  22.1 2.4 %gradients.1._.slopes = f32[2,256,16,128]{3,2,1,0:T(8,128)S(1)} custom-call(bf16[128,128]{1,0:T(8,128)(2,1)S(1)} %collective-permute-done.refs_1_.z_low_in, bf16[128,128]{1,0:T(8,128)(2,1)S(1)} %collective-permute-done.1.refs_2_.z_high_in, bf16[256,16,128]{2,1,0:T(8,128)(2,1)S(1)} %copy-done), custom_call_target="tpu_custom_call" | custom-call | tf_op jit(solution)/shard_map/gradients/pallas_call | solution.py:509
  24.5 0.0 copy-start.1
  24.5 0.0 copy-start.2
  24.5 0.0 copy-start.3
  24.5 2.8 %collective-permute-done.2.above_in = bf16[352,128]{1,0:T(8,128)(2,1)S(1)} collective-permute-done((bf16[352,128]{1,0:T(8,128)(2,1)S(1)}, bf16[352,128]{1,0:T(8,128)(2,1)S(1)}, u32[]{:S(2)}, u32[]{:S(2)}) %collective-permute-start.2) | collective-permute-done | bytes 90144 | tf_op jit(solution)/shard_map/ppermute | solution.py:505
  27.4 0.0 collective-permute-done.3.below_in
  27.4 0.0 copy-done.4
  27.4 0.4 right_hand_sides.1
  27.7 17.2 %all_to_all.5.slab_in = bf16[16,48,128]{2,1,0:T(8,128)(2,1)S(1)} all-to-all(bf16[16,48,128]{2,1,0:T(8,128)(2,1)S(1)} %get-tuple-element.23), channel_id=1, replica_groups=mesh['gx'=16,'gy'=4,'gz'=8] {'gx'}, dimensions={0} | all-to-all | bytes 393216 | tf_op jit(solution)/shard_map/all_to_all | solution.py:530
  44.9 0.0 copy-done.1
  45.0 0.0 copy-done.2
  45.0 0.0 copy-done.3
  45.0 3.7 %solve_and_residual.1 = (f32[3,2,16,32]{3,2,1,0:T(8,128)}, bf16[256,16,128]{2,1,0:T(8,128)(2,1)}) custom-call(bf16[16,48,128]{2,1,0:T(8,128)(2,1)S(1)} %all_to_all.5.slab_in, f32[3,32,128]{2,1,0:T(8,128)S(1)} %get-tuple-element.24.rhs_in, f32[3,32,128]{2,1,0:T(8,128)S(1)} %get-tuple-element.25.disp_in, f32[16,40,80]{2,1,0:T(8,128)S(1)} %copy-done.3, ...), custom_call_target="tpu_custom_call" | custom-call | tf_op jit(solution)/shard_map/solve_and_residual/pallas_call | solution.py:531
Async XLA Ops:
  0.6 26.7 %copy-start.4 = (f32[16,8,32]{2,1,0:T(8,128)S(1)}, f32[16,8,32]{2,1,0:T(8,128)}, u32[]{:S(2)}) copy-start(f32[16,8,32]{2,1,0:T(8,128)} %constant.6.clone.weights_in) | copy-start | bytes 49156
  0.6 0.8 %copy-start.5 = (f32[3,32,2,16]{1,3,2,0:T(8,128)S(1)}, f32[3,32,2,16]{1,3,2,0:T(8,128)}, u32[]{:S(2)}) copy-start(f32[3,32,2,16]{1,3,2,0:T(8,128)} %param.8) | copy-start | bytes 36868
  4.3 3.4 %collective-permute-start = (bf16[128,128]{1,0:T(8,128)(2,1)S(1)}, bf16[128,128]{1,0:T(8,128)(2,1)S(1)}, u32[]{:S(2)}, u32[]{:S(2)}) collective-permute-start(bf16[128,128]{1,0:T(8,128)(2,1)S(1)} %get-tuple-element.16), channel_id=1, source_target_pairs={{0,1},{1,2},{2,3},{3,4},{4,5},{5,6},{6,7},{7,0},{8,9},{9,10},{10,1... | collective-permute-start | bytes 98312 | tf_op jit(solution)/shard_map/ppermute | solution.py:491
  4.3 6.7 %collective-permute-start.1 = (bf16[128,128]{1,0:T(8,128)(2,1)S(1)}, bf16[128,128]{1,0:T(8,128)(2,1)S(1)}, u32[]{:S(2)}, u32[]{:S(2)}) collective-permute-start(bf16[128,128]{1,0:T(8,128)(2,1)S(1)} %get-tuple-element.17), channel_id=1, source_target_pairs={{1,0},{2,1},{3,2},{4,3},{5,4},{6,5},{7,6},{0,7},{9,8},{10,9},{11,1... | collective-permute-start | bytes 98312 | tf_op jit(solution)/shard_map/ppermute | solution.py:492
  11.1 16.2 %collective-permute-start.2 = (bf16[352,128]{1,0:T(8,128)(2,1)S(1)}, bf16[352,128]{1,0:T(8,128)(2,1)S(1)}, u32[]{:S(2)}, u32[]{:S(2)}) collective-permute-start(bf16[352,128]{1,0:T(8,128)(2,1)S(1)} %get-tuple-element.21), channel_id=1, source_target_pairs={{8,0},{16,8},{24,16},{9,1},{17,9},{25,17},{10,2},{18,10},{26,18},{... | collective-permute-start | bytes 270344 | tf_op jit(solution)/shard_map/ppermute | solution.py:505
  12.4 14.9 %collective-permute-start.3 = (bf16[352,128]{1,0:T(8,128)(2,1)S(1)}, bf16[352,128]{1,0:T(8,128)(2,1)S(1)}, u32[]{:S(2)}, u32[]{:S(2)}) collective-permute-start(bf16[352,128]{1,0:T(8,128)(2,1)S(1)} %get-tuple-element.22), channel_id=1, source_target_pairs={{0,8},{8,16},{16,24},{1,9},{9,17},{17,25},{2,10},{10,18},{18,26},{... | collective-permute-start | bytes 270344 | tf_op jit(solution)/shard_map/ppermute | solution.py:506
  20.9 1.2 %copy-start = (bf16[256,16,128]{2,1,0:T(8,128)(2,1)S(1)}, bf16[256,16,128]{2,1,0:T(8,128)(2,1)}, u32[]{:S(2)}) copy-start(bf16[256,16,128]{2,1,0:T(8,128)(2,1)} %ref_in.5) | copy-start | bytes 3145732
  24.5 20.5 %copy-start.1 = (bf16[256,16,128]{2,1,0:T(8,128)(2,1)S(1)}, bf16[256,16,128]{2,1,0:T(8,128)(2,1)}, u32[]{:S(2)}) copy-start(bf16[256,16,128]{2,1,0:T(8,128)(2,1)} %def_in.1) | copy-start | bytes 3145732
  24.5 20.4 %copy-start.2 = (bf16[128,2048]{1,0:T(8,128)(2,1)S(1)}, bf16[128,2048]{1,0:T(8,128)(2,1)}, u32[]{:S(2)}) copy-start(bf16[128,2048]{1,0:T(8,128)(2,1)} %constant.8.clone.prolong_in) | copy-start | bytes 1572868
  24.5 20.4 %copy-start.3 = (f32[16,40,80]{2,1,0:T(8,128)S(1)}, f32[16,40,80]{2,1,0:T(8,128)}, u32[]{:S(2)}) copy-start(f32[16,40,80]{2,1,0:T(8,128)} %constant.7.clone.table_in) | copy-start | bytes 614404
